TPU v7x, 512 devices: a whole 4x8x8 slice. The times are simulated.
512 devices in a mesh: dp: 32 (over z, x_hi, core), clus: 16 (over x_lo, y).
Axes of the slice: x: 4 (x_hi: 2, x_lo: 2; x = x_hi * 2 + x_lo), y: 8, z: 8, core: 2. Of those that a mesh axis runs over, the one named last changes fastest.
Arguments:
- rows: bfloat16 [131072, 1024], P(('dp', 'clus')), may hold values from -8 to 8
- fine_assign: int32 [131072], P(('dp', 'clus')), may hold values from 0 to 131071, as said below
- parent1: int32 [131072], P(('dp', 'clus')), may hold values from 0 to 8191, as said below
- parent2: int32 [8192], P('dp'), may hold values from 0 to 511
- parent3: int32 [512], replicated, may hold values from 0 to 63
- shrink: float32 [4], replicated, may hold values from 0.5 to 2
Outputs:
- fine_centroids: bfloat16 [131072, 1024], P(('dp', 'clus'))
- mid_centroids: bfloat16 [8192, 1024], P(('dp', 'clus'))
- coarse_centroids: bfloat16 [512, 1024], P(('dp', 'clus'))
- spread: float32 [131072], P(('dp', 'clus'))
Inputs may be any that keep to these rules, and one draw needn't show every extreme that they name: `fine_assign`: devices are numbered d = dp index * 16 + clus index, and fine centroid k is owned by device k // 256. Every row of device d names a fine centroid owned by a device of the same dp index. At most 32 rows of one device name centroids of one owner, and in every dp group some owner is named by exactly 32 rows of each device of the group. parent1[k] is one of the 256 second-level centroids g * 256 to g * 256 + 255, with g = k // 4096.
All inputs are finite; a program needn't handle non-finite values.
Results may differ from a plain program's by a relative error of at most 0.0035.
Values may be sent and summed in bfloat16 or wider, within the bound.
No kernel may reach another device: no remote copies, remote signals or barrier semaphores. Data moves between devices by JAX's collectives and lax.ppermute only.
A program may use at most 64 MiB of HBM per device.

v0:
```python
import math

import jax
import jax.numpy as jnp
from jax import lax
from jax.sharding import PartitionSpec as P

K4 = 64


HIGH = lax.Precision.HIGHEST


def split_up(x, dim, count):
    shape = x.shape
    parts = x.reshape(*shape[:dim], count, shape[dim] // count, *shape[dim + 1 :])
    return jnp.moveaxis(parts, dim, 0)


def sent_and_summed(x, axis, dim):
    parts = split_up(x, dim, lax.axis_size(axis))
    arrived = lax.all_to_all(parts, axis, split_axis=0, concat_axis=0, tiled=True)
    return arrived.sum(axis=0)


def in_one_piece(arrays, axis, dim, along):
    widths = [math.prod(a.shape[along:]) for a in arrays]
    both = jnp.concatenate(
        [a.reshape(*a.shape[:along], w) for a, w in zip(arrays, widths)], axis=along
    )
    whole = sent_and_summed(both, axis, dim)
    parts = jnp.split(whole, [sum(widths[:k]) for k in range(1, len(widths))], axis=along)
    return tuple((b.reshape(*whole.shape[:along], *a.shape[along:]) for a, b in zip(arrays, parts)))


def in_order(parts, dim):
    shape = list(parts.shape[1:])
    shape[dim] *= parts.shape[0]
    return jnp.moveaxis(parts, 0, dim).reshape(shape)


def copy_for_each(x, axis):
    copies = jnp.broadcast_to(x, (lax.axis_size(axis), *x.shape))
    return lax.all_to_all(copies, axis, split_axis=0, concat_axis=0, tiled=True)


def collect(x, axis, dim):
    return in_order(copy_for_each(x, axis), dim)


def shrunk(sums, counts, prior, weight):
    return (sums + weight * prior) / (counts + weight)[:, None]


def local(rows, fine_assign, parent1, parent2, parent3, shrink):
    groups = lax.axis_size("clus")
    dp_count = lax.axis_size("dp")
    devices = groups * dp_count
    clus_index = lax.axis_index("clus")
    dp_index = lax.axis_index("dp")
    count = rows.shape[0]
    width = rows.shape[1]
    fine_dev = parent1.shape[0]
    middle_dp = parent2.shape[0]
    third = parent3.shape[0]
    slots = 2 * count // groups
    total = count * devices
    weight_top = shrink[0] * (total / K4)
    weight_third = shrink[1] * (total / third)
    weight_middle = shrink[2] * (total / (middle_dp * dp_count))
    weight_fine = shrink[3] * (total / (fine_dev * devices))
    local_ids = fine_assign - dp_index * groups * fine_dev
    target = local_ids // fine_dev
    within = local_ids - target * fine_dev
    target_hot = (target[:, None] == jnp.arange(groups)[None, :]).astype(jnp.bfloat16)
    earlier = (jnp.arange(count)[:, None] > jnp.arange(count)[None, :]).astype(jnp.bfloat16)
    before = jnp.dot(earlier, target_hot, preferred_element_type=jnp.float32)
    rank = jnp.sum(before * target_hot.astype(jnp.float32), axis=1).astype(jnp.int32)
    slot_of = target * slots + rank
    source = (
        jnp.full((groups * slots,), count, jnp.int32)
        .at[slot_of]
        .set(jnp.arange(count, dtype=jnp.int32))
    )
    padded = jnp.concatenate([rows, jnp.zeros((1, width), jnp.bfloat16)], axis=0)
    send_rows = padded[source].reshape(groups, slots, width)
    send_ids = jnp.concatenate([within, jnp.full((1,), -1, jnp.int32)])[source].reshape(
        groups, slots
    )
    got_rows, got_ids = (
        lax.all_to_all(send_rows, "clus", split_axis=0, concat_axis=0, tiled=True),
        lax.all_to_all(send_ids, "clus", split_axis=0, concat_axis=0, tiled=True),
    )
    got_rows = got_rows.reshape(groups * slots, width)
    got_ids = got_ids.reshape(groups * slots)
    member = (got_ids[:, None] == jnp.arange(fine_dev)[None, :]).astype(jnp.bfloat16)
    contract = (((0,), (0,)), ((), ()))
    fine_sums = lax.dot_general(member, got_rows, contract, preferred_element_type=jnp.float32)
    fine_counts = jnp.sum(member.astype(jnp.float32), axis=0)
    middle_local = parent1 - dp_index * middle_dp
    child_hot = (jnp.arange(middle_dp)[:, None] == middle_local[None, :]).astype(jnp.float32)
    middle_part = jnp.dot(child_hot, fine_sums, precision=HIGH)
    middle_tally = jnp.dot(child_hot, fine_counts, precision=HIGH)
    share = middle_dp // groups
    offset = clus_index * share
    middle_sums, middle_counts = in_one_piece((middle_part, middle_tally), "clus", 0, 1)
    own_parent2 = lax.dynamic_slice_in_dim(parent2, offset, share, 0)
    third_share = third // devices
    third_start = (dp_index * groups + clus_index) * third_share
    third_hot = (jnp.arange(third)[:, None] == own_parent2[None, :]).astype(jnp.float32)
    third_part = jnp.dot(third_hot, middle_sums, precision=HIGH)
    third_tally = jnp.dot(third_hot, middle_counts, precision=HIGH)
    third_sums, third_counts = lax.psum((third_part, third_tally), ("dp", "clus"))
    top_hot = (jnp.arange(K4)[:, None] == parent3[None, :]).astype(jnp.float32)
    top_sums = jnp.dot(top_hot, third_sums, precision=HIGH)
    top_counts = jnp.dot(top_hot, third_counts, precision=HIGH)
    center = jnp.sum(top_sums, axis=0) / total
    top_means = shrunk(top_sums, top_counts, center[None, :], weight_top)
    third_means = shrunk(
        third_sums, third_counts, jnp.dot(top_hot.T, top_means, precision=HIGH), weight_third
    )
    third_out = lax.dynamic_slice_in_dim(third_means, third_start, third_share, 0)
    parent_hot = (own_parent2[:, None] == jnp.arange(third)[None, :]).astype(jnp.float32)
    middle_out = shrunk(
        middle_sums, middle_counts, jnp.dot(parent_hot, third_means, precision=HIGH), weight_middle
    )
    middle_means = collect(middle_out, "clus", 0)
    fine_means = shrunk(
        fine_sums, fine_counts, jnp.dot(child_hot.T, middle_means, precision=HIGH), weight_fine
    )
    fine_out = fine_means.astype(jnp.bfloat16)
    back = jnp.dot(member, fine_out, preferred_element_type=jnp.float32)
    diff = got_rows.astype(jnp.float32) - back
    row_error = jnp.sum(diff * diff, axis=1)
    spread = jnp.sum(member.astype(jnp.float32) * row_error[:, None], axis=0) / (
        width * (fine_counts + 1.0)
    )
    return (fine_out, middle_out.astype(jnp.bfloat16), third_out.astype(jnp.bfloat16), spread)


def solution(mesh):
    placed = (P(("dp", "clus"), None), P(("dp", "clus")), P(("dp", "clus")), P("dp"), P(), P())
    return jax.shard_map(
        local,
        mesh=mesh,
        in_specs=placed,
        out_specs=(
            P(("dp", "clus"), None),
            P(("dp", "clus"), None),
            P(("dp", "clus"), None),
            P(("dp", "clus")),
        ),
        check_vma=False,
    )
```

profile of v0, /device:TPU:8, one launch (start us, length us, event | category | flops | bytes accessed | tf_op | source)
XLA Modules:
  0.0 429.1 jit_solution(13146403856222873392)
XLA Ops:
  7.2 0.7 multiply_subtract_fusion
  8.2 1.4 scatter_custom_fusion
  9.6 3.5 gather_fusion
  13.8 9.1 %all-to-all-start = ((s32[16,1,32]{2,1,0:T(1,128)}), s32[16,1,32]{2,1,0:T(1,128)S(1)}, u32[]{:S(2)}, u32[]{:S(2)}) async-start(s32[16,1,32]{2,1,0:T(1,128)} %all_to_all.15), calls=%async_computation | async-start | bytes 16384 | tf_op jit(solution)/shard_map/all_to_all | solution.py:92
  22.9 2.8 gather_fusion.1
  25.7 4.3 all-to-all-done
  30.0 4.9 %all-to-all-start.1 = ((bf16[16,32,1024]{2,1,0:T(8,128)(2,1)}), bf16[16,32,1024]{2,1,0:T(8,128)(2,1)S(1)}, u32[]{:S(2)}, u32[]{:S(2)}) async-start(bf16[16,32,1024]{2,1,0:T(8,128)(2,1)} %bitcast), calls=%async_computation.1 | async-start | bytes 2097152 | tf_op jit(solution)/shard_map/all_to_all | solution.py:91
  36.6 22.8 %all-to-all-done.1 = bf16[16,32,1024]{2,1,0:T(8,128)(2,1)S(1)} async-done(((bf16[16,32,1024]{2,1,0:T(8,128)(2,1)}), bf16[16,32,1024]{2,1,0:T(8,128)(2,1)S(1)}, u32[]{:S(2)}, u32[]{:S(2)}) %all-to-all-start.1) | async-done | bytes 1048608 | tf_op jit(solution)/shard_map/all_to_all | solution.py:91
  60.0 0.7 fusion.14
  60.7 1.1 pad_maximum_fusion
  61.9 5.2 %all-to-all-start.2 = ((f32[16,16,1025]{2,1,0:T(8,128)}), f32[16,16,1025]{2,1,0:T(8,128)S(1)}, u32[]{:S(2)}, u32[]{:S(2)}) async-start(f32[16,16,1025]{2,1,0:T(8,128)} %pad_maximum_fusion), calls=%async_computation.2 | async-start | bytes 2359296 | tf_op jit(solution)/shard_map/all_to_all | solution.py:22
  67.2 26.9 %all-to-all-done.2 = f32[16,16,1025]{2,1,0:T(8,128)S(1)} async-done(((f32[16,16,1025]{2,1,0:T(8,128)}), f32[16,16,1025]{2,1,0:T(8,128)S(1)}, u32[]{:S(2)}, u32[]{:S(2)}) %all-to-all-start.2) | async-done | bytes 1049632 | tf_op jit(solution)/shard_map/all_to_all | solution.py:22
  94.2 2.3 fusion.13
  100.0 103.9 %psum.15 = f32[512]{0:T(512)S(1)} all-reduce(f32[512]{0:T(512)S(1)} %bitcast.38), channel_id=1, replica_groups=mesh['dp'=32,'clus'=16] {'dp','clus'}, use_global_device_ids=true, to_apply=%region_6.7 | all-reduce | flops 512 | bytes 4096 | tf_op jit(solution)/shard_map/psum | solution.py:113
  204.1 174.4 %all-reduce.3.cloned.1.call-done = f32[512,1024]{1,0:T(8,128)} async-done(((f32[512,1024]{1,0:T(8,128)}), f32[512,1024]{1,0:T(8,128)}) %all-reduce.3.cloned.1.call-update) | async-done | bytes 2097168 | tf_op jit(solution)/shard_map/psum | solution.py:113
  378.5 2.7 fusion.38
  381.2 1.2 add_divide_fusion
  382.4 1.3 copy-done
  383.7 1.4 fusion.39
  385.1 1.1 broadcast_in_dim.11
  386.2 7.9 %all-to-all-start.3 = ((f32[16,16,1024]{2,1,0:T(8,128)}), f32[16,16,1024]{2,1,0:T(8,128)S(1)}, u32[]{:S(2)}, u32[]{:S(2)}) async-start(f32[16,16,1024]{2,1,0:T(8,128)} %broadcast_in_dim.11), calls=%async_computation.3 | async-start | bytes 2097152 | tf_op jit(solution)/shard_map/all_to_all | solution.py:44
  394.8 1.4 dynamic-slice_convert_fusion
  396.2 23.3 %all-to-all-done.3 = f32[16,16,1024]{2,1,0:T(8,128)S(1)} async-done(((f32[16,16,1024]{2,1,0:T(8,128)}), f32[16,16,1024]{2,1,0:T(8,128)S(1)}, u32[]{:S(2)}, u32[]{:S(2)}) %all-to-all-start.3) | async-done | bytes 1048608 | tf_op jit(solution)/shard_map/all_to_all | solution.py:44
  419.4 1.4 fusion.2
  (45 shorter events, 6.6 us)
Async XLA Ops:
  7.2 15.7 %copy-start.2 = (bf16[256,1024]{1,0:T(8,128)(2,1)S(1)}, bf16[256,1024]{1,0:T(8,128)(2,1)}, u32[]{:S(2)}) copy-start(bf16[256,1024]{1,0:T(8,128)(2,1)} %param.6) | copy-start | bytes 1572868
  13.8 16.2 %all-to-all-start = ((s32[16,1,32]{2,1,0:T(1,128)}), s32[16,1,32]{2,1,0:T(1,128)S(1)}, u32[]{:S(2)}, u32[]{:S(2)}) async-start(s32[16,1,32]{2,1,0:T(1,128)} %all_to_all.15), calls=%async_computation | async-start | bytes 16384 | tf_op jit(solution)/shard_map/all_to_all | solution.py:92
  25.7 9.2 %copy-start.5 = (s32[256]{0:T(256)S(1)}, s32[256]{0:T(256)}, u32[]{:S(2)}) copy-start(s32[256]{0:T(256)} %param.8) | copy-start | bytes 3076
  30.0 29.5 %all-to-all-start.1 = ((bf16[16,32,1024]{2,1,0:T(8,128)(2,1)}), bf16[16,32,1024]{2,1,0:T(8,128)(2,1)S(1)}, u32[]{:S(2)}, u32[]{:S(2)}) async-start(bf16[16,32,1024]{2,1,0:T(8,128)(2,1)} %bitcast), calls=%async_computation.1 | async-start | bytes 2097152 | tf_op jit(solution)/shard_map/all_to_all | solution.py:91
  60.7 6.3 %copy-start.6 = (s32[256]{0:T(256)S(1)}, s32[256]{0:T(256)}, u32[]{:S(2)}) copy-start(s32[256]{0:T(256)} %param.9) | copy-start | bytes 3076
  61.9 32.2 %all-to-all-start.2 = ((f32[16,16,1025]{2,1,0:T(8,128)}), f32[16,16,1025]{2,1,0:T(8,128)S(1)}, u32[]{:S(2)}, u32[]{:S(2)}) async-start(f32[16,16,1025]{2,1,0:T(8,128)} %pad_maximum_fusion), calls=%async_computation.2 | async-start | bytes 2359296 | tf_op jit(solution)/shard_map/all_to_all | solution.py:22
  67.0 311.4 %all-reduce.3.cloned.1.call-start = ((), (), s32[]{:S(2)}) async-start(), calls=%async_computation.4 | async-start | bytes 4194304 | tf_op jit(solution)/shard_map/psum | solution.py:113
  94.1 2.3 copy-start.3
  94.1 109.8 %copy-start.4 = (s32[512]{0:T(512)S(1)}, s32[512]{0:T(512)}, u32[]{:S(2)}) copy-start(s32[512]{0:T(512)} %param.10) | copy-start | bytes 6148
  378.5 2.7 copy-start.1
  382.4 1.4 copy-start
  386.2 33.2 %all-to-all-start.3 = ((f32[16,16,1024]{2,1,0:T(8,128)}), f32[16,16,1024]{2,1,0:T(8,128)S(1)}, u32[]{:S(2)}, u32[]{:S(2)}) async-start(f32[16,16,1024]{2,1,0:T(8,128)} %broadcast_in_dim.11), calls=%async_computation.3 | async-start | bytes 2097152 | tf_op jit(solution)/shard_map/all_to_all | solution.py:44
  420.8 1.4 copy-start.7
Sparse Core Ops, SparseCore 0:
  96.6 281.8 all-reduce.2
where the time goes:
time: 430 us; the launch traced here: 429 us
  waiting for transfers between devices  252 us (59%)
  blocking collectives  104 us (24%)
  starting transfers between devices  27.1 us (6%)
  between operations  16.9 us (4%)
  local copies, waits for them, and re-layouts  13.5 us (3%)
  matrix products  11.6 us (3%)
  other arithmetic  4.36 us (1%)
    psum x1, waiting for transfers between devices, local(): lax.psum((third_part, third_tally), ('dp', 'clus'))  174 us
    psum x1, blocking collectives, local(): lax.psum((third_part, third_tally), ('dp', 'clus'))  104 us
    all_to_all x1, waiting for transfers between devices, sent_and_summed(): lax.all_to_all(parts, axis, split_axis=0, concat_axis=0, tiled=True)  26.9 us
    all_to_all x1, waiting for transfers between devices, copy_for_each(): return lax.all_to_all(copies, axis, split_axis=0, concat_axis=0, tiled=True)  23.3 us
    all_to_all x1, waiting for transfers between devices, local(): lax.all_to_all(send_rows, 'clus', split_axis=0, concat_axis=0, tiled=True)  22.8 us
    all_to_all x1, starting transfers between devices, local(): lax.all_to_all(send_ids, 'clus', split_axis=0, concat_axis=0, tiled=True)  9.08 us
  transfers between devices with their start and end apart: 5, of which 5 were waited for; matrix products, arithmetic and copies ran while one was open for 2% of the time, Pallas kernels for 0%

commit v1 on v0

v1 whole, which is shorter than its diff:
```python
import jax
import jax.numpy as jnp
from jax import lax
from jax.experimental import pallas as pl
from jax.experimental.pallas import tpu as pltpu
from jax.sharding import PartitionSpec as P

GROUPS = 16
DP = 32
FINE = 256
MIDDLE = 256
THIRD = 512
TOP = 64
WIDTH = 1024
PART = WIDTH // GROUPS
TOTAL = 131072.0
BF = jnp.bfloat16
F32 = jnp.float32
I32 = jnp.int32
LIMIT = 24 * 1024 * 1024


def iota(shape, dim):
    return lax.broadcasted_iota(I32, shape, dim)


def hot(mask):
    return jnp.where(mask, 1.0, 0.0).astype(BF)


def pieces(x, count):
    out = []
    for k in range(count):
        part = x.astype(BF)
        out.append(part)
        if k + 1 < count:
            x = x - part.astype(F32)
    return out


def turned(x):
    return pltpu.roll(x, PART, 1)


def dot(a, b):
    return jnp.dot(a, b, preferred_element_type=F32)


def dot_first(a, b):
    return lax.dot_general(a, b, (((0,), (0,)), ((), ())), preferred_element_type=F32)


def summed(x, count):
    total = x[:, 0:128]
    for k in range(1, count):
        total = total + x[:, 128 * k : 128 * (k + 1)]
    return total


def in_line(ref, first, count):
    return jnp.concatenate([ref[first + k : first + k + 1, :] for k in range(count)], axis=1)


def pack_kernel(rows_ref, assign_ref, parent1_ref, send_ref, ids_ref):
    left = iota((128, 128), 1) < PART
    for g in range(GROUPS // 2):
        top = rows_ref[0:128, 128 * g : 128 * (g + 1)].astype(F32)
        low = rows_ref[128:256, 128 * g : 128 * (g + 1)].astype(F32)
        send_ref[2 * g] = jnp.where(left, top, turned(low)).astype(BF)
        send_ref[2 * g + 1] = jnp.where(left, turned(top), low).astype(BF)
    fine = (assign_ref[...] & (GROUPS * FINE - 1)).astype(F32)
    parent = (parent1_ref[...] & (MIDDLE - 1)).astype(F32)
    tile = jnp.concatenate([fine, parent, jnp.zeros((4, 128), F32)], axis=0)
    ids_ref[...] = jnp.broadcast_to(tile[None], (GROUPS, 8, 128))


def middle_kernel(rows_ref, ids_ref, parent2_ref, third_ref, middle_ref, tally_ref, hot_ref):
    left = iota((256, 128), 1) < PART
    table = jnp.concatenate([ids_ref[:, 2, :], ids_ref[:, 3, :]], axis=1).astype(BF)
    down = iota((256, 128), 0)
    owner = iota((GROUPS, 128), 0)
    for s in range(GROUPS):
        for j in range(2):
            fine = ids_ref[s, j : j + 1, :].astype(I32)
            found = dot(table, hot(down == (fine & (FINE - 1))))
            parent = jnp.sum(jnp.where(owner == (fine >> 8), found, 0.0), axis=0, keepdims=True)
            hot_ref[256 * j : 256 * (j + 1), 128 * s : 128 * (s + 1)] = hot(
                down == parent.astype(I32)
            )
    both = dot(hot_ref[...], rows_ref[...].reshape(GROUPS * 128, 128))
    middle = jnp.where(left, both[0:256], both[256:512])
    middle = middle + turned(middle)
    ones = jnp.ones((GROUPS * 128, 128), BF)
    tally = dot(hot_ref[0:256] + hot_ref[256:512], ones)
    middle_ref[...] = middle
    tally_ref[...] = tally
    line = in_line(parent2_ref, 0, 2)
    third = iota((256, 256), 0)
    parts = jnp.concatenate(pieces(middle, 3) + pieces(tally, 2), axis=1)
    first = dot(hot(third == line), parts)
    second = dot(hot(third + 256 == line), parts)
    sums = jnp.where(left, summed(first, 3), summed(second, 3))
    counts = jnp.where(left, summed(first[:, 384:], 2), summed(second[:, 384:], 2))
    third_ref[:, 0:8, :] = sums.reshape(DP, 8, 128)
    third_ref[:, 8:16, :] = counts.reshape(DP, 8, 128)


def fine_kernel(shrink_ref, rows_ref, ids_ref, sums_ref, inv_ref, count_ref, lines_ref, hot_ref, wide_ref, acc_ref):
    lane = iota((128, 128), 1)
    left = lane < PART
    half = jnp.where(left, 0, 1)
    group = lane >> 5
    down = iota((128, 128), 0)
    weight = shrink_ref[3]
    columns = jnp.transpose(ids_ref[...].reshape(128, 128)).astype(I32)
    for s in range(GROUPS):
        x = rows_ref[s].astype(F32)
        y = turned(x)
        ones = []
        for j in range(2):
            block = slice(128 * j, 128 * (j + 1))
            twice = jnp.where(left, x, y) if j == 0 else jnp.where(left, y, x)
            key = columns[:, 8 * s + j : 8 * s + j + 1] >> 7
            place = jnp.broadcast_to(key, (128, 128)) - half
            for h in range(GROUPS):
                wide_ref[block, 128 * h : 128 * (h + 1)] = jnp.where(
                    place == 2 * h, twice, 0.0
                ).astype(BF)
            square = 0.5 * jnp.sum(twice * twice, axis=1, keepdims=True)
            hi, mid, lo = [p.astype(F32) for p in pieces(jnp.broadcast_to(square, (128, 128)), 3)]
            value = jnp.where(group == 0, hi, jnp.where(group == 1, mid, jnp.where(group == 2, lo, 1.0)))
            wide_ref[block, 2048:2176] = jnp.where((lane & 31) == key, value, 0.0).astype(BF)
            fine = ids_ref[s, j : j + 1, :].astype(I32)
            ones.append(hot(down == (fine & 127)))
        part = dot(jnp.concatenate(ones, axis=1), wide_ref[...])
        acc_ref[...] = part if s == 0 else acc_ref[...] + part
    sums_ref[...] = acc_ref[:, 0:2048]
    tail = acc_ref[:, 2048:2176]
    square = tail[:, 0:32] + tail[:, 32:64] + tail[:, 64:96]
    count = tail[:, 96:128]
    lines_ref[...] = jnp.transpose(
        jnp.concatenate([square, count, jnp.zeros((128, 64), F32)], axis=1)
    )
    inverse = 1.0 / (count + weight)
    across = iota((128, 256), 1)
    for h in range(GROUPS):
        here = slice(128 * h, 128 * (h + 1))
        inv_ref[:, here] = jnp.where(left, inverse[:, 2 * h : 2 * h + 1], inverse[:, 2 * h + 1 : 2 * h + 2])
        count_ref[:, here] = jnp.where(left, count[:, 2 * h : 2 * h + 1], count[:, 2 * h + 1 : 2 * h + 2])
        for b in range(2):
            parent = columns[:, 8 * h + 2 + b : 8 * h + 3 + b]
            hot_ref[256 * h + 128 * b : 256 * h + 128 * (b + 1), :] = hot(across == parent)


def spread_out_kernel(got_ref, out_ref):
    total = got_ref[0]
    for k in range(1, DP):
        total = total + got_ref[k]
    out_ref[...] = jnp.broadcast_to(total[None], (DP, 16, 128))


def down_kernel(
    shrink_ref, dp_ref, got_ref, parent2_ref, parent3_ref, middle_ref, tally_ref, sums_ref, inv_ref,
    count_ref, lines_ref, hot_ref, fine_ref, small_ref, third_ref, diff_ref,
):
    left = iota((256, 128), 1) < PART
    weight_top = shrink_ref[0] * (TOTAL / TOP)
    weight_third = shrink_ref[1] * (TOTAL / THIRD)
    weight_middle = shrink_ref[2] * (TOTAL / 8192)
    weight_fine = shrink_ref[3]
    third_sums = got_ref[:, 0:8, :].reshape(256, 128)
    third_counts = got_ref[:, 8:16, :].reshape(256, 128)
    top_id = iota((TOP, 256), 0)
    hot_first = hot(top_id == in_line(parent3_ref, 0, 2))
    hot_second = hot(top_id == in_line(parent3_ref, 2, 2))
    parts = jnp.concatenate(pieces(third_sums, 3) + pieces(third_counts, 3), axis=1)
    first = dot(hot_first, parts)
    second = dot(hot_second, parts)
    top = jnp.where(left[0:TOP], summed(first, 3), summed(second, 3))
    top = top + turned(top)
    top_counts = jnp.where(left[0:TOP], summed(first[:, 384:], 3), summed(second[:, 384:], 3))
    top_counts = top_counts + turned(top_counts)
    center = jnp.sum(top, axis=0, keepdims=True) / TOTAL
    top_means = (top + weight_top * center) / (top_counts + weight_top)
    parts = jnp.concatenate(pieces(top_means, 3), axis=1)
    prior = jnp.where(
        left, summed(dot_first(hot_first, parts), 3), summed(dot_first(hot_second, parts), 3)
    )
    third_means = (third_sums + weight_third * prior) / (third_counts + weight_third)
    third_ref[...] = third_means
    line = in_line(parent2_ref, 0, 2)
    third_id = iota((256, 256), 0)
    parts = jnp.concatenate(pieces(third_means, 3), axis=1)
    prior = jnp.where(
        left,
        summed(dot_first(hot(third_id == line), parts), 3),
        summed(dot_first(hot(third_id + 256 == line), parts), 3),
    )
    prior = prior + turned(prior)
    middle_means = (middle_ref[...] + weight_middle * prior) / (tally_ref[...] + weight_middle)
    parts = jnp.concatenate(pieces(middle_means, 2), axis=1)
    left = left[0:128]
    for h in range(GROUPS):
        here = slice(128 * h, 128 * (h + 1))
        found = summed(dot(hot_ref[256 * h : 256 * (h + 1), :], parts), 2)
        prior = jnp.where(left, found[0:128], found[128:256])
        sums = sums_ref[:, here]
        fine = ((sums + weight_fine * prior) * inv_ref[:, here]).astype(BF)
        fine_ref[h] = fine
        fine = fine.astype(F32)
        hi, lo = pieces(fine * (count_ref[:, here] * fine - 2.0 * sums), 2)
        diff_ref[:, here] = hi
        diff_ref[:, 2048 + 128 * h : 2048 + 128 * (h + 1)] = lo
    select = hot((iota((2048, 128), 0) >> 6) == iota((2048, 128), 1))
    diff = dot(diff_ref[:, 0:2048], select) + dot(diff_ref[:, 2048:4096], select)
    spread = jnp.transpose(diff)[0:32] + lines_ref[0:32]
    counts = lines_ref[32:64]
    dp = dp_ref[0]
    own = third_ref[pl.ds(pl.multiple_of((dp % 16) * 16, 16), 16), :]
    own = jnp.where(dp < 16, own, turned(own))
    for h in range(GROUPS):
        small_ref[h, 0:8, :] = jnp.where(
            left[0:8], middle_means[16 * h : 16 * h + 8], middle_means[16 * h + 8 : 16 * h + 16]
        )
        small_ref[h, 8:16, :] = jnp.concatenate(
            [
                own[h : h + 1],
                spread[2 * h : 2 * h + 2],
                counts[2 * h : 2 * h + 2],
                jnp.zeros((3, 128), F32),
            ],
            axis=0,
        )


def finish_kernel(fine_ref, small_ref, out_ref, middle_ref, third_ref, spread_ref):
    left = iota((128, 128), 1) < PART
    for g in range(GROUPS // 2):
        here = slice(128 * g, 128 * (g + 1))
        a = fine_ref[2 * g].astype(F32)
        b = fine_ref[2 * g + 1].astype(F32)
        out_ref[0:128, here] = jnp.where(left, a, turned(b)).astype(BF)
        out_ref[128:256, here] = jnp.where(left, turned(a), b).astype(BF)
        a = small_ref[2 * g]
        b = small_ref[2 * g + 1]
        first = jnp.where(left[0:16], a, turned(b))
        second = jnp.where(left[0:16], turned(a), b)
        middle_ref[:, here] = jnp.concatenate([first[0:8], second[0:8]], axis=0).astype(BF)
        third_ref[:, here] = first[8:9].astype(BF)
    total = small_ref[0, 8:16, :]
    counts = total[3:5]
    for k in range(1, GROUPS):
        total = total + small_ref[k, 8:16, :]
    spread_ref[...] = total[1:3] / (WIDTH * (counts + 1.0))


VMEM = pl.BlockSpec(memory_space=pltpu.VMEM)
SMEM = pl.BlockSpec(memory_space=pltpu.SMEM)


def call(kernel, ins, outs, scratch=(), cost=(0, 0)):
    return pl.pallas_call(
        kernel,
        out_shape=[jax.ShapeDtypeStruct(s, d) for s, d in outs],
        in_specs=ins,
        out_specs=[VMEM] * len(outs),
        scratch_shapes=[pltpu.VMEM(s, d) for s, d in scratch],
        compiler_params=pltpu.CompilerParams(vmem_limit_bytes=LIMIT),
        cost_estimate=pl.CostEstimate(flops=cost[0], bytes_accessed=cost[1], transcendentals=0),
    )


def exchange(x, axis):
    return lax.all_to_all(x, axis, split_axis=0, concat_axis=0, tiled=True)


def local(rows, fine_assign, parent1, parent2, parent3, shrink):
    dp = lax.axis_index("dp").astype(I32).reshape(1)
    parent2 = parent2.reshape(2, 128)
    parent3 = parent3.reshape(4, 128)
    send, ids = call(
        pack_kernel, [VMEM] * 3, [((GROUPS, 128, 128), BF), ((GROUPS, 8, 128), F32)]
    )(rows, fine_assign.reshape(2, 128), parent1.reshape(2, 128))
    ids = exchange(ids, "clus")
    group_rows = exchange(send, "clus")
    third, middle, tally = call(
        middle_kernel,
        [VMEM] * 3,
        [((DP, 16, 128), F32), ((256, 128), F32), ((256, 128), F32)],
        [((512, 2048), BF)],
    )(group_rows, ids, parent2)
    third = exchange(third, "dp")
    sums, inverse, counts, lines, parents = call(
        fine_kernel,
        [SMEM, VMEM, VMEM],
        [((128, 2048), F32), ((128, 2048), F32), ((128, 2048), F32), ((128, 128), F32), ((4096, 256), BF)],
        [((256, 2176), BF), ((128, 2176), F32)],
        (4_000_000_000, 4_000_000),
    )(shrink, group_rows, ids)
    (third,) = call(spread_out_kernel, [VMEM], [((DP, 16, 128), F32)])(third)
    third = exchange(third, "dp")
    fine, small = call(
        down_kernel,
        [SMEM, SMEM] + [VMEM] * 10,
        [((GROUPS, 128, 128), BF), ((GROUPS, 16, 128), F32)],
        [((256, 128), F32), ((128, 4096), BF)],
    )(shrink, dp, third, parent2, parent3, middle, tally, sums, inverse, counts, lines, parents)
    fine = exchange(fine, "clus")
    small = exchange(small, "clus")
    fine, middle, third, spread = call(
        finish_kernel,
        [VMEM] * 2,
        [((256, 1024), BF), ((16, 1024), BF), ((1, 1024), BF), ((2, 128), F32)],
    )(fine, small)
    return fine, middle, third, spread.reshape(256)


def solution(mesh):
    placed = (P(("dp", "clus"), None), P(("dp", "clus")), P(("dp", "clus")), P("dp"), P(), P())
    return jax.shard_map(
        local,
        mesh=mesh,
        in_specs=placed,
        out_specs=(
            P(("dp", "clus"), None),
            P(("dp", "clus"), None),
            P(("dp", "clus"), None),
            P(("dp", "clus")),
        ),
        check_vma=False,
    )
```

time: 430 us -> 124 us (0.29)
  the two profiles are of different devices: /device:TPU:8 before, /device:TPU:14 now
where the time goes in v1:
time: 124 us
  blocking collectives  90.5 us (73%)
  Pallas kernels  17.7 us (14%)
  local copies, waits for them, and re-layouts  9.68 us (8%)
  starting transfers between devices  4.99 us (4%)
    all_to_all x5, blocking collectives, exchange(): return lax.all_to_all(x, axis, split_axis=0, concat_axis=0, tiled=True)  90.5 us
    pallas_call x1, Pallas kernels, local(): call(fine_kernel, [SMEM, VMEM, VMEM], [((128, 2048), F32), ((128, 2048),...  10.4 us
    unnamed x26, local copies, waits for them, and re-layouts  9.68 us
    all_to_all x1, starting transfers between devices, exchange(): return lax.all_to_all(x, axis, split_axis=0, concat_axis=0, tiled=True)  4.99 us
    pallas_call x1, Pallas kernels, local(): call(down_kernel, [SMEM, SMEM] + [VMEM] * 10, [((GROUPS, 128, 128), BF),...  2.95 us
  transfers between devices with their start and end apart: 1, of which 0 were waited for; matrix products, arithmetic and copies ran while one was open for 0% of the time, Pallas kernels for 8%

profile of v1, /device:TPU:14, one launch (start us, length us, event | category | flops | bytes accessed | tf_op | source)
XLA Modules:
  0.0 123.6 jit_solution(13971488093161650265)
XLA Ops:
  0.7 1.0 copy-done.6
  1.7 0.7 copy-done.10
  2.4 0.7 copy-done.11
  3.0 0.2 shard_map.93
  3.3 15.1 %all_to_all.30.ids_ref = f32[16,8,128]{2,1,0:T(8,128)S(1)} all-to-all(f32[16,8,128]{2,1,0:T(8,128)S(1)} %get-tuple-element.21), channel_id=1, replica_groups=mesh['dp'=32,'clus'=16] {'clus'}, dimensions={0} | all-to-all | bytes 131072 | tf_op jit(solution)/shard_map/all_to_all | solution.py:274
  18.4 18.5 %all_to_all.31.rows_ref = bf16[16,128,128]{2,1,0:T(8,128)(2,1)S(1)} all-to-all(bf16[16,128,128]{2,1,0:T(8,128)(2,1)S(1)} %get-tuple-element.20), channel_id=1, replica_groups=mesh['dp'=32,'clus'=16] {'clus'}, dimensions={0} | all-to-all | bytes 1048576 | tf_op jit(solution)/shard_map/all_to_all | solution.py:274
  36.9 0.7 copy-done.7
  37.5 2.4 %shard_map.94 = (f32[32,16,128]{2,1,0:T(8,128)S(1)}, f32[256,128]{1,0:T(8,128)S(1)}, f32[256,128]{1,0:T(8,128)S(1)}) custom-call(bf16[16,128,128]{2,1,0:T(8,128)(2,1)S(1)} %all_to_all.31.rows_ref, f32[16,8,128]{2,1,0:T(8,128)S(1)} %all_to_all.30.ids_ref, s32[2,128]{1,0:T(2,128)S(1)} %bitcast.6), custom_call_target="tpu_custom_call" | custom-call | tf_op jit(solution)/shard_map/pallas_call | solution.py:286
  39.9 25.3 %all_to_all.32.got_ref = f32[32,16,128]{2,1,0:T(8,128)S(1)} all-to-all(f32[32,16,128]{2,1,0:T(8,128)S(1)} %get-tuple-element.22), channel_id=1, replica_groups=mesh['dp'=32,'clus'=16] {'dp'}, dimensions={0} | all-to-all | bytes 524288 | tf_op jit(solution)/shard_map/all_to_all | solution.py:274
  65.2 0.8 shard_map.95
  66.0 5.0 %all-to-all-start.3 = ((f32[32,16,128]{2,1,0:T(8,128)}), f32[32,16,128]{2,1,0:T(8,128)S(1)}, u32[]{:S(2)}, u32[]{:S(2)}) async-start(f32[32,16,128]{2,1,0:T(8,128)} %shard_map.95), calls=%async_computation.3 | async-start | bytes 524288 | tf_op jit(solution)/shard_map/all_to_all | solution.py:274
  71.0 0.0 copy-start.8
  71.0 0.0 copy-start.9
  71.0 10.4 %shard_map.96 = (f32[128,2048]{1,0:T(8,128)S(1)}, f32[128,2048]{1,0:T(8,128)S(1)}, f32[128,2048]{1,0:T(8,128)S(1)}, f32[128,128]{1,0:T(8,128)S(1)}, bf16[4096,256]{1,0:T(8,128)(2,1)S(1)}) custom-call(f32[4]{0:T(128)S(1)} %copy-done.12, bf16[16,128,128]{2,1,0:T(8,128)(2,1)S(1)} %all_to_all.31.rows_ref, f32[16,8,128]{2,1,0:T(8,128)S(1)} %all_to_all.30.ids_ref), custom_call_target="tpu_custom_call" | custom-call | flops 4000000000 | bytes 4000000 | tf_op jit(solution)/shard_map/pallas_call | solution.py:293
  81.4 1.0 copy-done
  82.4 1.0 copy-done.2
  83.4 1.0 copy-done.4
  84.4 1.2 copy-done.1
  85.6 1.2 copy-done.3
  86.8 1.2 copy-done.5
  88.0 2.9 %shard_map.97 = (bf16[16,128,128]{2,1,0:T(8,128)(2,1)S(1)}, f32[16,16,128]{2,1,0:T(8,128)S(1)}) custom-call(f32[4]{0:T(128)S(1)} %copy-done.12, s32[1]{0:T(128)} %bitcast.dp_ref, f32[32,16,128]{2,1,0:T(8,128)S(1)} %all-to-all-done.3.got_ref, s32[2,128]{1,0:T(2,128)S(1)} %bitcast.7, s32[4,128]{1,0:T(4,128)S(1)} %bitcast.8, ...), custom_call_target="tpu_custom_call" | custom-call | tf_op jit(solution)/shard_map/pallas_call | solution.py:302
  91.0 12.5 %all_to_all.33.small_ref = f32[16,16,128]{2,1,0:T(8,128)S(1)} all-to-all(f32[16,16,128]{2,1,0:T(8,128)S(1)} %get-tuple-element.31), channel_id=1, replica_groups=mesh['dp'=32,'clus'=16] {'clus'}, dimensions={0} | all-to-all | bytes 262144 | tf_op jit(solution)/shard_map/all_to_all | solution.py:274
  103.4 19.1 %all_to_all.34.fine_ref = bf16[16,128,128]{2,1,0:T(8,128)(2,1)S(1)} all-to-all(bf16[16,128,128]{2,1,0:T(8,128)(2,1)S(1)} %get-tuple-element.30), channel_id=1, replica_groups=mesh['dp'=32,'clus'=16] {'clus'}, dimensions={0} | all-to-all | bytes 1048576 | tf_op jit(solution)/shard_map/all_to_all | solution.py:274
  122.6 1.1 shard_map.98
  (15 shorter events, 0.0 us)
Async XLA Ops:
  0.6 70.3 %copy-start.12 = (f32[4]{0:T(128)S(1)}, f32[4]{0:T(128)}, u32[]{:S(2)}) copy-start(f32[4]{0:T(128)} %shrink_ref.3) | copy-start | bytes 52
  0.6 1.0 copy-start.6
  1.7 0.7 copy-start.10
  2.4 0.7 copy-start.11
  36.9 0.7 copy-start.7
  66.0 18.4 %all-to-all-start.3 = ((f32[32,16,128]{2,1,0:T(8,128)}), f32[32,16,128]{2,1,0:T(8,128)S(1)}, u32[]{:S(2)}, u32[]{:S(2)}) async-start(f32[32,16,128]{2,1,0:T(8,128)} %shard_map.95), calls=%async_computation.3 | async-start | bytes 524288 | tf_op jit(solution)/shard_map/all_to_all | solution.py:274
  71.0 13.4 %copy-start.8 = (s32[256]{0:T(256)S(1)}, s32[256]{0:T(256)}, u32[]{:S(2)}) copy-start(s32[256]{0:T(256)} %param.9) | copy-start | bytes 3076
  71.0 13.3 %copy-start.9 = (s32[512]{0:T(512)S(1)}, s32[512]{0:T(512)}, u32[]{:S(2)}) copy-start(s32[512]{0:T(512)} %param.10) | copy-start | bytes 6148
  81.4 1.0 copy-start
  82.4 1.0 copy-start.2
  83.4 1.0 copy-start.4
  84.3 1.2 copy-start.1
  85.6 1.2 copy-start.3
  86.8 1.2 copy-start.5

commit v2 on v1

v2 whole, which is shorter than its diff:
```python
import jax
import jax.numpy as jnp
from jax import lax
from jax.experimental import pallas as pl
from jax.experimental.pallas import tpu as pltpu
from jax.sharding import PartitionSpec as P

GROUPS = 16
DP = 32
FINE = 256
MIDDLE = 256
THIRD = 512
TOP = 64
WIDTH = 1024
PART = WIDTH // GROUPS
ROWS = 144
TOTAL = 131072.0
BF = jnp.bfloat16
F32 = jnp.float32
I32 = jnp.int32
MIB = 1024 * 1024


def iota(shape, dim):
    return lax.broadcasted_iota(I32, shape, dim)


def hot(mask):
    return jnp.where(mask, 1.0, 0.0).astype(BF)


def pieces(x, count):
    out = []
    for k in range(count):
        part = x.astype(BF)
        out.append(part)
        if k + 1 < count:
            x = x - part.astype(F32)
    return out


def side(x, count):
    return jnp.concatenate(pieces(x, count), axis=1)


def turned(x):
    return pltpu.roll(x, PART, 1)


def dot(a, b):
    return jnp.dot(a, b, preferred_element_type=F32)


def dot_last(a, b):
    return lax.dot_general(a, b, (((1,), (1,)), ((), ())), preferred_element_type=F32)


def two(x):
    return x[:, 0:128] + x[:, 128:256]


def in_line(ref, first, count):
    return jnp.concatenate([ref[first + k : first + k + 1, :] for k in range(count)], axis=1)


def pack_kernel(rows_hbm, assign_hbm, parent1_hbm, send_ref, rows_ref, assign_ref, parent1_ref, sems):
    copies = [
        pltpu.make_async_copy(src, dst, sems.at[k])
        for k, (src, dst) in enumerate(
            [(rows_hbm, rows_ref), (assign_hbm, assign_ref), (parent1_hbm, parent1_ref)]
        )
    ]
    for copy in copies:
        copy.start()
    copies[1].wait()
    copies[2].wait()
    fine = assign_ref[...] & (GROUPS * FINE - 1)
    parent = parent1_ref[...] & (MIDDLE - 1)
    tile = jnp.concatenate(
        [
            (fine >> 8).astype(F32),
            (fine & (FINE - 1)).astype(F32),
            parent.astype(F32),
            jnp.zeros((10, 128), F32),
        ],
        axis=0,
    ).astype(BF)
    for k in range(GROUPS):
        send_ref[k, 128:144, :] = tile
    copies[0].wait()
    left = iota((128, 128), 1) < PART
    for g in range(GROUPS // 2):
        top = rows_ref[0:128, 128 * g : 128 * (g + 1)].astype(F32)
        low = rows_ref[128:256, 128 * g : 128 * (g + 1)].astype(F32)
        send_ref[2 * g, 0:128, :] = jnp.where(left, top, turned(low)).astype(BF)
        send_ref[2 * g + 1, 0:128, :] = jnp.where(left, turned(top), low).astype(BF)


def middle_kernel(rows_ref, parent2_hbm, third_ref, middle_ref, line_ref, ids_ref, hot_ref, parent2_ref, sem):
    copy = pltpu.make_async_copy(parent2_hbm, parent2_ref, sem)
    copy.start()
    left = iota((256, 128), 1) < PART
    tails = [rows_ref[s, 128:144, :].astype(F32)[0:8] for s in range(GROUPS)]
    for s in range(GROUPS):
        ids_ref[8 * s : 8 * s + 8, :] = tails[s]
    table = jnp.concatenate(
        [jnp.concatenate([tail[k : k + 1] for tail in tails], axis=0) for k in (4, 5)], axis=1
    ).astype(BF)
    down = iota((256, 128), 0)
    owner = iota((GROUPS, 128), 0)
    for s in range(GROUPS):
        tail = tails[s].astype(I32)
        for j in range(2):
            found = dot(table, hot(down == tail[2 + j : 3 + j]))
            parent = jnp.sum(jnp.where(owner == tail[j : j + 1], found, 0.0), axis=0, keepdims=True)
            hot_ref[256 * j : 256 * (j + 1), 128 * s : 128 * (s + 1)] = hot(
                down == parent.astype(I32)
            )
    both = dot(hot_ref[...], rows_ref[:, 0:128, :].reshape(GROUPS * 128, 128))
    middle = jnp.where(left, both[0:256], both[256:512])
    middle = middle + turned(middle)
    tally = dot_last(jnp.ones((8, 2048), BF), hot_ref[0:256] + hot_ref[256:512])
    middle_ref[...] = middle
    line_ref[...] = tally
    copy.wait()
    line = in_line(parent2_ref, 0, 2)
    third = iota((256, 256), 0)
    first = hot(third == line)
    second = hot(third + 256 == line)
    parts = side(middle, 2)
    sums = jnp.where(left, two(dot(first, parts)), two(dot(second, parts))).reshape(DP, 8, 128)
    third_ref[:, 0] = sums[:, 0:4]
    third_ref[:, 1] = sums[:, 4:8]
    high, low = pieces(tally, 2)
    for k, ones in enumerate((first, second)):
        count = dot_last(high, ones) + dot_last(low, ones)
        for i in range(2):
            third_ref[:, 2, 2 * k + i, :] = jnp.broadcast_to(
                count[0:1, 128 * i : 128 * (i + 1)], (DP, 128)
            )


def fine_kernel(rows_ref, ids_ref, acc_ref, wide_ref):
    lane = iota((128, 128), 1)
    left = lane < PART
    half = jnp.where(left, 0.0, 1.0)
    group = lane >> 5
    down = iota((128, 128), 0)
    columns = jnp.transpose(ids_ref[...])
    for s in range(GROUPS):
        x = rows_ref[s, 0:128, :].astype(F32)
        y = turned(x)
        ones = []
        for j in range(2):
            block = slice(128 * j, 128 * (j + 1))
            twice = jnp.where(left, x, y) if j == 0 else jnp.where(left, y, x)
            low = columns[:, 8 * s + 2 + j : 8 * s + 3 + j]
            key = 2.0 * columns[:, 8 * s + j : 8 * s + j + 1] + jnp.where(low >= 128.0, 1.0, 0.0)
            key = jnp.broadcast_to(key, (128, 128))
            place = (key - half).astype(BF)
            narrow = twice.astype(BF)
            for h in range(GROUPS):
                wide_ref[block, 128 * h : 128 * (h + 1)] = jnp.where(
                    place == jnp.array(2 * h, BF), narrow, jnp.array(0, BF)
                )
            square = 0.5 * jnp.sum(twice * twice, axis=1, keepdims=True)
            hi, mid, lo = [p.astype(F32) for p in pieces(jnp.broadcast_to(square, (128, 128)), 3)]
            value = jnp.where(group == 0, hi, jnp.where(group == 1, mid, jnp.where(group == 2, lo, 1.0)))
            wide_ref[block, 2048:2176] = jnp.where(
                (lane & 31) == key.astype(I32), value, 0.0
            ).astype(BF)
            within = ids_ref[8 * s + 2 + j : 8 * s + 3 + j, :].astype(I32) & 127
            ones.append(hot(down == within))
        part = dot(jnp.concatenate(ones, axis=1), wide_ref[...])
        acc_ref[...] = part if s == 0 else acc_ref[...] + part


def share_kernel(got_ref, acc_hbm, out_ref, count_ref):
    total = got_ref[0]
    for k in range(1, DP):
        total = total + got_ref[k]
    sums = jnp.concatenate([total[0], total[1]], axis=0)
    out_ref[...] = jnp.broadcast_to(sums[None], (DP, 8, 128))
    count_ref[...] = total[2]


def ready_kernel(
    shrink_ref, acc_ref, ids_ref, line_ref, third_ref, parent2_ref, parent3_ref, inv_ref, count_ref,
    lines_ref, hot_ref, third_inv_ref, top_inv_ref, middle_inv_ref, top_hot_ref, top_turn_ref, middle_turn_ref,
):
    weight_top = shrink_ref[0] * (TOTAL / TOP)
    weight_third = shrink_ref[1] * (TOTAL / THIRD)
    weight_middle = shrink_ref[2] * (TOTAL / 8192)
    weight_fine = shrink_ref[3]
    left = iota((256, 128), 1) < PART
    columns = jnp.transpose(ids_ref[...])
    tail = acc_ref[:, 2048:2176]
    square = tail[:, 0:32] + tail[:, 32:64] + tail[:, 64:96]
    count = tail[:, 96:128]
    lines_ref[...] = jnp.transpose(
        jnp.concatenate([square, count, jnp.zeros((128, 64), F32)], axis=1)
    )
    inverse = 1.0 / (count + weight_fine)
    across = iota((128, 256), 1)
    for h in range(GROUPS):
        here = slice(128 * h, 128 * (h + 1))
        pair = (slice(2 * h, 2 * h + 1), slice(2 * h + 1, 2 * h + 2))
        inv_ref[:, here] = jnp.where(left[0:128], inverse[:, pair[0]], inverse[:, pair[1]])
        count_ref[:, here] = jnp.where(left[0:128], count[:, pair[0]], count[:, pair[1]])
        for b in range(2):
            parent = columns[:, 8 * h + 4 + b : 8 * h + 5 + b].astype(I32)
            hot_ref[256 * h + 128 * b : 256 * h + 128 * (b + 1), :] = hot(across == parent)
    tally = line_ref[0:1, :]
    lines = jnp.concatenate(
        [
            third_ref[...],
            tally[:, 0:128],
            tally[:, 128:256],
            parent2_ref[...].astype(F32),
            parent3_ref[...].astype(F32),
            jnp.zeros((116, 128), F32),
        ],
        axis=0,
    )
    columns = jnp.transpose(lines)
    first = jnp.concatenate([columns[:, 0:1], columns[:, 1:2]], axis=0)
    second = jnp.concatenate([columns[:, 2:3], columns[:, 3:4]], axis=0)
    counts = jnp.where(left, first, second)
    third_inv_ref[...] = 1.0 / (counts + weight_third)
    tally = jnp.concatenate([columns[:, 4:5], columns[:, 5:6]], axis=0)
    middle_inv_ref[...] = jnp.broadcast_to(1.0 / (tally + weight_middle), (256, 128))
    top_id = iota((TOP, 256), 0)
    top_first = hot(top_id == in_line(parent3_ref, 0, 2))
    top_second = hot(top_id == in_line(parent3_ref, 2, 2))
    top_hot_ref[0:TOP, :] = top_first
    top_hot_ref[TOP : 2 * TOP, :] = top_second
    parts = jnp.concatenate(pieces(counts, 3), axis=1)
    first = dot(top_first, parts)
    second = dot(top_second, parts)
    first = first[:, 0:128] + first[:, 128:256] + first[:, 256:384]
    second = second[:, 0:128] + second[:, 128:256] + second[:, 256:384]
    top = jnp.where(left[0:TOP], first, second)
    top_inv_ref[...] = 1.0 / (top + turned(top) + weight_top)
    parents = [columns[:, 6 + k : 7 + k].astype(I32) for k in range(6)]
    for k in range(2):
        for b in range(2):
            middle_turn_ref[256 * b + 128 * k : 256 * b + 128 * (k + 1), :] = hot(
                across + 256 * b == parents[k]
            )
    for k in range(4):
        top_turn_ref[128 * k : 128 * (k + 1), :] = hot(across[:, 0:128] == parents[2 + k])[:, 0:TOP]


def down_kernel(
    shrink_ref, dp_ref, got_ref, middle_ref, acc_ref, inv_ref, count_ref, lines_ref, hot_ref, third_inv_ref,
    top_inv_ref, middle_inv_ref, top_hot_ref, top_turn_ref, middle_turn_ref, send_ref, third_ref, diff_ref,
):
    left = iota((256, 128), 1) < PART
    weight_top = shrink_ref[0] * (TOTAL / TOP)
    weight_third = shrink_ref[1] * (TOTAL / THIRD)
    weight_middle = shrink_ref[2] * (TOTAL / 8192)
    weight_fine = shrink_ref[3]
    third_sums = got_ref[...].reshape(256, 128)
    top = two(dot(top_hot_ref[...], side(third_sums, 2)))
    top = jnp.where(left[0:TOP], top[0:TOP], top[TOP : 2 * TOP])
    top = top + turned(top)
    center = jnp.sum(top, axis=0, keepdims=True) / TOTAL
    top_means = (top + weight_top * center) * top_inv_ref[...]
    prior = two(dot(top_turn_ref[...], side(top_means, 2)))
    prior = jnp.where(left, prior[0:256], prior[256:512])
    third_means = (third_sums + weight_third * prior) * third_inv_ref[...]
    third_ref[...] = third_means
    prior = two(dot(middle_turn_ref[...], side(third_means, 2)))
    prior = jnp.where(left, prior[0:256], prior[256:512])
    prior = prior + turned(prior)
    middle_means = (middle_ref[...] + weight_middle * prior) * middle_inv_ref[...]
    parts = side(middle_means, 2)
    left = left[0:128]
    for h in range(GROUPS):
        here = slice(128 * h, 128 * (h + 1))
        found = two(dot(hot_ref[256 * h : 256 * (h + 1), :], parts))
        prior = jnp.where(left, found[0:128], found[128:256])
        sums = acc_ref[:, here]
        fine = ((sums + weight_fine * prior) * inv_ref[:, here]).astype(BF)
        send_ref[h, 0:128, :] = fine
        fine = fine.astype(F32)
        hi, lo = pieces(fine * (count_ref[:, here] * fine - 2.0 * sums), 2)
        diff_ref[:, here] = hi
        diff_ref[:, 2048 + 128 * h : 2048 + 128 * (h + 1)] = lo
    select = hot((iota((2048, 128), 0) >> 6) == iota((2048, 128), 1))
    diff = dot(diff_ref[:, 0:2048], select) + dot(diff_ref[:, 2048:4096], select)
    spread = jnp.transpose(diff)[0:32] + lines_ref[0:32]
    spread = [p.astype(F32) for p in pieces(spread, 3)]
    dp = dp_ref[0]
    own = third_ref[pl.ds(pl.multiple_of((dp % 16) * 16, 16), 16), :]
    own = jnp.where(dp < 16, own, turned(own))
    for h in range(GROUPS):
        send_ref[h, 128:144, :] = jnp.concatenate(
            [
                jnp.where(
                    left[0:8], middle_means[16 * h : 16 * h + 8], middle_means[16 * h + 8 : 16 * h + 16]
                ),
                own[h : h + 1],
                spread[0][2 * h : 2 * h + 2],
                spread[1][2 * h : 2 * h + 2],
                spread[2][2 * h : 2 * h + 2],
                jnp.zeros((1, 128), F32),
            ],
            axis=0,
        ).astype(BF)


def finish_kernel(clus_ref, got_ref, lines_ref, out_ref, middle_ref, third_ref, spread_ref):
    left = iota((128, 128), 1) < PART
    total = jnp.zeros((8, 128), F32)
    for g in range(GROUPS // 2):
        here = slice(128 * g, 128 * (g + 1))
        a = got_ref[2 * g, 0:128, :].astype(F32)
        b = got_ref[2 * g + 1, 0:128, :].astype(F32)
        out_ref[0:128, here] = jnp.where(left, a, turned(b)).astype(BF)
        out_ref[128:256, here] = jnp.where(left, turned(a), b).astype(BF)
        a = got_ref[2 * g, 128:144, :].astype(F32)
        b = got_ref[2 * g + 1, 128:144, :].astype(F32)
        first = jnp.where(left[0:16], a, turned(b))
        second = jnp.where(left[0:16], turned(a), b)
        middle_ref[:, here] = jnp.concatenate([first[0:8], second[0:8]], axis=0).astype(BF)
        third_ref[:, here] = first[8:9].astype(BF)
        total = total + a[8:16] + b[8:16]
    total = total[1:3] + total[3:5] + total[5:7]
    row = iota((32, 128), 0)
    counts = [
        jnp.sum(jnp.where(row == 2 * clus_ref[0] + b, lines_ref[32:64], 0.0), axis=0, keepdims=True)
        for b in range(2)
    ]
    spread_ref[...] = total / (WIDTH * (jnp.concatenate(counts, axis=0) + 1.0))


VMEM = pl.BlockSpec(memory_space=pltpu.VMEM)
SMEM = pl.BlockSpec(memory_space=pltpu.SMEM)
ANY = pl.BlockSpec(memory_space=pl.ANY)
DMA = pltpu.SemaphoreType.DMA


def call(kernel, limit, ins, outs, scratch=(), flops=0, moved=0):
    return pl.pallas_call(
        kernel,
        out_shape=[jax.ShapeDtypeStruct(s, d) for s, d in outs],
        in_specs=ins,
        out_specs=[VMEM] * len(outs),
        scratch_shapes=list(scratch),
        compiler_params=pltpu.CompilerParams(vmem_limit_bytes=limit * MIB),
        cost_estimate=pl.CostEstimate(flops=flops, bytes_accessed=moved, transcendentals=0),
    )


def exchange(x, axis):
    return lax.all_to_all(x, axis, split_axis=0, concat_axis=0, tiled=True)


def local(rows, fine_assign, parent1, parent2, parent3, shrink):
    dp = lax.axis_index("dp").astype(I32).reshape(1)
    clus = lax.axis_index("clus").astype(I32).reshape(1)
    parent2 = parent2.reshape(2, 128)
    parent3 = parent3.reshape(4, 128)
    block = ((GROUPS, ROWS, 128), BF)
    (send,) = call(
        pack_kernel,
        60,
        [ANY] * 3,
        [block],
        [
            pltpu.VMEM((256, WIDTH), BF),
            pltpu.VMEM((2, 128), I32),
            pltpu.VMEM((2, 128), I32),
            DMA((3,)),
        ],
    )(rows, fine_assign.reshape(2, 128), parent1.reshape(2, 128))
    group_rows = exchange(send, "clus")
    third, middle, line, ids = call(
        middle_kernel,
        32,
        [VMEM, ANY],
        [((DP, 3, 4, 128), F32), ((256, 128), F32), ((8, 256), F32), ((128, 128), F32)],
        [pltpu.VMEM((512, 2048), BF), pltpu.VMEM((2, 128), I32), DMA],
    )(group_rows, parent2)
    third = exchange(third, "dp")
    (sums,) = call(
        fine_kernel,
        32,
        [VMEM, VMEM],
        [((128, 2176), F32)],
        [pltpu.VMEM((256, 2176), BF)],
        4_000_000_000,
        4_000_000,
    )(group_rows, ids)
    third, counts = call(
        share_kernel,
        16, [VMEM, ANY], [((DP, 8, 128), F32), ((4, 128), F32)]
    )(third, sums)
    third = exchange(third, "dp")
    ready = call(
        ready_kernel,
        60,
        [SMEM] + [VMEM] * 6,
        [
            ((128, 2048), F32),
            ((128, 2048), F32),
            ((128, 128), F32),
            ((4096, 256), BF),
            ((256, 128), F32),
            ((TOP, 128), F32),
            ((256, 128), F32),
            ((2 * TOP, 256), BF),
            ((THIRD, TOP), BF),
            ((2 * MIDDLE, 256), BF),
        ],
        (),
        1_000_000_000,
        8_000_000,
    )(shrink, sums, ids, line, counts, parent2, parent3)
    (send,) = call(
        down_kernel,
        59,
        [SMEM, SMEM] + [VMEM] * 13,
        [block],
        [pltpu.VMEM((256, 128), F32), pltpu.VMEM((128, 4096), BF)],
    )(shrink, dp, third, middle, sums, *ready)
    got = exchange(send, "clus")
    fine, middle, third, spread = call(
        finish_kernel,
        16,
        [SMEM, VMEM, VMEM],
        [((256, 1024), BF), ((16, 1024), BF), ((1, 1024), BF), ((2, 128), F32)],
    )(clus, got, ready[2])
    return fine, middle, third, spread.reshape(256)


def solution(mesh):
    placed = (P(("dp", "clus"), None), P(("dp", "clus")), P(("dp", "clus")), P("dp"), P(), P())
    return jax.shard_map(
        local,
        mesh=mesh,
        in_specs=placed,
        out_specs=(
            P(("dp", "clus"), None),
            P(("dp", "clus"), None),
            P(("dp", "clus"), None),
            P(("dp", "clus")),
        ),
        check_vma=False,
    )
```

time: 124 us -> 105 us (0.85)
  the two profiles are of different devices: /device:TPU:14 before, /device:TPU:10 now
where the time goes in v2:
time: 105 us; the launch traced here: 104 us
  waiting for transfers between devices  27.9 us (27%)
  blocking collectives  25.8 us (25%)
  Pallas kernels  24.9 us (24%)
  starting transfers between devices  22.8 us (22%)
  local copies, waits for them, and re-layouts  1.91 us (2%)
    all_to_all x3, waiting for transfers between devices, exchange(): return lax.all_to_all(x, axis, split_axis=0, concat_axis=0, tiled=True)  27.9 us
    all_to_all x1, blocking collectives, exchange(): return lax.all_to_all(x, axis, split_axis=0, concat_axis=0, tiled=True)  25.8 us
    all_to_all x3, starting transfers between devices, exchange(): return lax.all_to_all(x, axis, split_axis=0, concat_axis=0, tiled=True)  22.8 us
    pallas_call x1, Pallas kernels, local(): call(fine_kernel, 32, [VMEM, VMEM], [((128, 2176), F32)], [pltpu.VMEM((25...  6.6 us
    pallas_call x1, Pallas kernels, local(): call(down_kernel, 59, [SMEM, SMEM] + [VMEM] * 13, [block], [pltpu.VMEM((2...  5.89 us
    pallas_call x1, Pallas kernels, local(): call(ready_kernel, 60, [SMEM] + [VMEM] * 6, [((128, 2048), F32), ((128, 2...  5.56 us
    pallas_call x1, Pallas kernels, local(): call(middle_kernel, 32, [VMEM, ANY], [((DP, 3, 4, 128), F32), ((256, 128)...  2.94 us
    pallas_call x1, Pallas kernels, local(): call(pack_kernel, 60, [ANY] * 3, [block], [pltpu.VMEM((256, WIDTH), BF),...  2.11 us
  transfers between devices with their start and end apart: 3, of which 3 were waited for; matrix products, arithmetic and copies ran while one was open for 0% of the time, Pallas kernels for 12%

profile of v2, /device:TPU:10, one launch (start us, length us, event | category | flops | bytes accessed | tf_op | source)
XLA Modules:
  0.0 104.1 jit_solution(18174182855289018806)
XLA Ops:
  0.6 0.0 copy-start.3
  0.6 2.1 %shard_map.93 = bf16[16,144,128]{2,1,0:T(8,128)(2,1)} custom-call(bf16[256,1024]{1,0:T(8,128)(2,1)} %rows_hbm.1, s32[2,128]{1,0:T(2,128)} %bitcast.9, s32[2,128]{1,0:T(2,128)} %bitcast.10), custom_call_target="tpu_custom_call" | custom-call | tf_op jit(solution)/shard_map/pallas_call | solution.py:366
  2.8 25.8 %all_to_all.20.rows_ref = bf16[16,144,128]{2,1,0:T(8,128)(2,1)S(1)} all-to-all(bf16[16,144,128]{2,1,0:T(8,128)(2,1)} %shard_map.93), channel_id=1, replica_groups=mesh['dp'=32,'clus'=16] {'clus'}, dimensions={0} | all-to-all | bytes 1179648 | tf_op jit(solution)/shard_map/all_to_all | solution.py:357
  28.6 0.0 copy-done.3
  28.6 2.9 %shard_map.94 = (f32[32,3,4,128]{3,2,1,0:T(4,128)}, f32[256,128]{1,0:T(8,128)S(1)}, f32[8,256]{1,0:T(8,128)S(1)}, f32[128,128]{1,0:T(8,128)S(1)}) custom-call(bf16[16,144,128]{2,1,0:T(8,128)(2,1)S(1)} %all_to_all.20.rows_ref, s32[2,128]{1,0:T(2,128)S(1)} %bitcast.8), custom_call_target="tpu_custom_call" | custom-call | tf_op jit(solution)/shard_map/pallas_call | solution.py:379
  31.5 0.0 copy-start.2
  31.5 0.6 copy-done.2
  32.2 0.6 copy-done.5
  32.8 12.3 %all-to-all-start.1 = ((f32[32,3,4,128]{3,2,1,0:T(4,128)}), f32[32,3,4,128]{3,2,1,0:T(4,128)S(1)}, u32[]{:S(2)}, u32[]{:S(2)}) async-start(f32[32,3,4,128]{3,2,1,0:T(4,128)} %get-tuple-element.24), calls=%async_computation.1 | async-start | bytes 393216 | tf_op jit(solution)/shard_map/all_to_all | solution.py:357
  45.1 6.6 %shard_map.95.acc_hbm.acc_ref = f32[128,2176]{1,0:T(8,128)S(1)} custom-call(bf16[16,144,128]{2,1,0:T(8,128)(2,1)S(1)} %all_to_all.20.rows_ref, f32[128,128]{1,0:T(8,128)S(1)} %get-tuple-element.25.ids_ref), custom_call_target="tpu_custom_call" | custom-call | flops 4000000000 | bytes 4000000 | tf_op jit(solution)/shard_map/pallas_call | solution.py:387
  51.7 0.0 copy-done.4
  51.7 0.0 copy-start
  51.7 5.4 %all-to-all-done.1.got_ref = f32[32,3,4,128]{3,2,1,0:T(4,128)S(1)} async-done(((f32[32,3,4,128]{3,2,1,0:T(4,128)}), f32[32,3,4,128]{3,2,1,0:T(4,128)S(1)}, u32[]{:S(2)}, u32[]{:S(2)}) %all-to-all-start.1) | async-done | bytes 196640 | tf_op jit(solution)/shard_map/all_to_all | solution.py:357
  57.1 0.7 shard_map.96
  57.8 4.7 %all-to-all-start.2 = ((f32[32,8,128]{2,1,0:T(8,128)}), f32[32,8,128]{2,1,0:T(8,128)S(1)}, u32[]{:S(2)}, u32[]{:S(2)}) async-start(f32[32,8,128]{2,1,0:T(8,128)} %get-tuple-element.26), calls=%async_computation.2 | async-start | bytes 262144 | tf_op jit(solution)/shard_map/all_to_all | solution.py:357
  62.5 0.0 copy-done
  62.5 0.0 copy-done.6
  62.5 5.6 %shard_map.97 = (f32[128,2048]{1,0:T(8,128)}, f32[128,2048]{1,0:T(8,128)}, f32[128,128]{1,0:T(8,128)}, bf16[4096,256]{1,0:T(8,128)(2,1)}, f32[256,128]{1,0:T(8,1...) custom-call(f32[4]{0:T(128)} %shrink_ref.3, ...), custom_call_target="tpu_custom_call" | custom-call | flops 1000000000 | bytes 8000000 | tf_op jit(solution)/shard_map/pallas_call | solution.py:401
  68.0 5.0 %all-to-all-done.2.got_ref = f32[32,8,128]{2,1,0:T(8,128)S(1)} async-done(((f32[32,8,128]{2,1,0:T(8,128)}), f32[32,8,128]{2,1,0:T(8,128)S(1)}, u32[]{:S(2)}, u32[]{:S(2)}) %all-to-all-start.2) | async-done | bytes 131104 | tf_op jit(solution)/shard_map/all_to_all | solution.py:357
  73.0 0.7 copy-done.7
  73.7 5.9 %shard_map.98 = bf16[16,144,128]{2,1,0:T(8,128)(2,1)} custom-call(f32[4]{0:T(128)} %shrink_ref.3, s32[1]{0:T(128)} %bitcast.1.dp_ref, f32[32,8,128]{2,1,0:T(8,128)} %copy-done.7, f32[256,128]{1,0:T(8,128)} %copy-done.2, f32[128,2176]{1,0:T(8,128)} %copy-done, f32[128,2048]{1,0:T(8,128)} %get-tuple-element.30.inv_ref, ...), custom_call_target="tpu_custom_call" | custom-call | tf_op jit(solution)/shard_map/pallas_call | solution.py:421
  79.6 5.9 %all-to-all-start.3 = ((bf16[16,144,128]{2,1,0:T(8,128)(2,1)}), bf16[16,144,128]{2,1,0:T(8,128)(2,1)S(1)}, u32[]{:S(2)}, u32[]{:S(2)}) async-start(bf16[16,144,128]{2,1,0:T(8,128)(2,1)} %shard_map.98), calls=%async_computation.3 | async-start | bytes 1179648 | tf_op jit(solution)/shard_map/all_to_all | solution.py:357
  85.5 17.5 %all-to-all-done.3.got_ref = bf16[16,144,128]{2,1,0:T(8,128)(2,1)S(1)} async-done(((bf16[16,144,128]{2,1,0:T(8,128)(2,1)}), bf16[16,144,128]{2,1,0:T(8,128)(2,1)S(1)}, u32[]{:S(2)}, u32[]{:S(2)}) %all-to-all-start.3) | async-done | bytes 589856 | tf_op jit(solution)/shard_map/all_to_all | solution.py:357
  103.0 1.1 %shard_map.99 = (bf16[256,1024]{1,0:T(8,128)(2,1)}, bf16[16,1024]{1,0:T(8,128)(2,1)}, bf16[1,1024]{1,0:T(2,128)(2,1)}, f32[2,128]{1,0:T(2,128)}) custom-call(s32[1]{0:T(128)} %bitcast.clus_ref, bf16[16,144,128]{2,1,0:T(8,128)(2,1)S(1)} %all-to-all-done.3.got_ref, f32[128,128]{1,0:T(8,128)S(1)} %copy-done.1), custom_call_target="tpu_custom_call" | custom-call | tf_op jit(solution)/shard_map/pallas_call | solution.py:429
  (6 shorter events, 0.0 us)
Async XLA Ops:
  0.6 28.0 %copy-start.3 = (s32[256]{0:T(256)S(1)}, s32[256]{0:T(256)}, u32[]{:S(2)}) copy-start(s32[256]{0:T(256)} %param.9) | copy-start | bytes 3076
  31.5 0.6 copy-start.2
  32.2 0.6 copy-start.5
  32.8 18.9 %copy-start.4 = (f32[128,128]{1,0:T(8,128)}, f32[128,128]{1,0:T(8,128)S(1)}, u32[]{:S(2)}) copy-start(f32[128,128]{1,0:T(8,128)S(1)} %get-tuple-element.25.ids_ref) | copy-start | bytes 196612
  32.8 24.3 %all-to-all-start.1 = ((f32[32,3,4,128]{3,2,1,0:T(4,128)}), f32[32,3,4,128]{3,2,1,0:T(4,128)S(1)}, u32[]{:S(2)}, u32[]{:S(2)}) async-start(f32[32,3,4,128]{3,2,1,0:T(4,128)} %get-tuple-element.24), calls=%async_computation.1 | async-start | bytes 393216 | tf_op jit(solution)/shard_map/all_to_all | solution.py:357
  51.7 10.8 %copy-start = (f32[128,2176]{1,0:T(8,128)}, f32[128,2176]{1,0:T(8,128)S(1)}, u32[]{:S(2)}) copy-start(f32[128,2176]{1,0:T(8,128)S(1)} %shard_map.95.acc_hbm.acc_ref) | copy-start | bytes 3342340
  57.8 4.7 %copy-start.6 = (f32[4,128]{1,0:T(4,128)}, f32[4,128]{1,0:T(4,128)S(1)}, u32[]{:S(2)}) copy-start(f32[4,128]{1,0:T(4,128)S(1)} %get-tuple-element.29.third_ref) | copy-start | bytes 6148
  57.8 15.3 %all-to-all-start.2 = ((f32[32,8,128]{2,1,0:T(8,128)}), f32[32,8,128]{2,1,0:T(8,128)S(1)}, u32[]{:S(2)}, u32[]{:S(2)}) async-start(f32[32,8,128]{2,1,0:T(8,128)} %get-tuple-element.26), calls=%async_computation.2 | async-start | bytes 262144 | tf_op jit(solution)/shard_map/all_to_all | solution.py:357
  73.0 0.7 copy-start.7
  73.7 29.3 %copy-start.1 = (f32[128,128]{1,0:T(8,128)S(1)}, f32[128,128]{1,0:T(8,128)}, u32[]{:S(2)}) copy-start(f32[128,128]{1,0:T(8,128)} %get-tuple-element.32.lines_ref) | copy-start | bytes 196612
  79.6 23.4 %all-to-all-start.3 = ((bf16[16,144,128]{2,1,0:T(8,128)(2,1)}), bf16[16,144,128]{2,1,0:T(8,128)(2,1)S(1)}, u32[]{:S(2)}, u32[]{:S(2)}) async-start(bf16[16,144,128]{2,1,0:T(8,128)(2,1)} %shard_map.98), calls=%async_computation.3 | async-start | bytes 1179648 | tf_op jit(solution)/shard_map/all_to_all | solution.py:357

commit v3 on v2

--- a/solution.py
+++ b/solution.py
@@ -27,6 +27,12 @@
 
 def hot(mask):
     return jnp.where(mask, 1.0, 0.0).astype(BF)
+
+
+def hot_row(down, row):
+    return jnp.where(
+        down == jnp.broadcast_to(row.astype(BF), down.shape), jnp.array(1, BF), jnp.array(0, BF)
+    )
 
 
 def pieces(x, count):
@@ -96,32 +102,32 @@
         send_ref[2 * g + 1, 0:128, :] = jnp.where(left, turned(top), low).astype(BF)
 
 
-def middle_kernel(rows_ref, parent2_hbm, third_ref, middle_ref, line_ref, ids_ref, hot_ref, parent2_ref, sem):
+def middle_kernel(rows_ref, parent2_hbm, third_ref, middle_ref, hot_ref, parent2_ref, sem):
     copy = pltpu.make_async_copy(parent2_hbm, parent2_ref, sem)
     copy.start()
     left = iota((256, 128), 1) < PART
     tails = [rows_ref[s, 128:144, :].astype(F32)[0:8] for s in range(GROUPS)]
-    for s in range(GROUPS):
-        ids_ref[8 * s : 8 * s + 8, :] = tails[s]
     table = jnp.concatenate(
         [jnp.concatenate([tail[k : k + 1] for tail in tails], axis=0) for k in (4, 5)], axis=1
     ).astype(BF)
-    down = iota((256, 128), 0)
-    owner = iota((GROUPS, 128), 0)
+    down = iota((256, 256), 0).astype(F32).astype(BF)
+    owner = iota((GROUPS, 256), 0).astype(F32)
     for s in range(GROUPS):
-        tail = tails[s].astype(I32)
-        for j in range(2):
-            found = dot(table, hot(down == tail[2 + j : 3 + j]))
-            parent = jnp.sum(jnp.where(owner == tail[j : j + 1], found, 0.0), axis=0, keepdims=True)
-            hot_ref[256 * j : 256 * (j + 1), 128 * s : 128 * (s + 1)] = hot(
-                down == parent.astype(I32)
-            )
+        tail = tails[s]
+        high = jnp.concatenate([tail[0:1], tail[1:2]], axis=1)
+        low = jnp.concatenate([tail[2:3], tail[3:4]], axis=1)
+        found = dot(table, hot_row(down, low))
+        parent = jnp.sum(jnp.where(owner == high, found, 0.0), axis=0, keepdims=True)
+        ones = hot_row(down, parent)
+        hot_ref[0:256, 128 * s : 128 * (s + 1)] = ones[:, 0:128]
+        hot_ref[256:512, 128 * s : 128 * (s + 1)] = ones[:, 128:256]
     both = dot(hot_ref[...], rows_ref[:, 0:128, :].reshape(GROUPS * 128, 128))
     middle = jnp.where(left, both[0:256], both[256:512])
     middle = middle + turned(middle)
     tally = dot_last(jnp.ones((8, 2048), BF), hot_ref[0:256] + hot_ref[256:512])
-    middle_ref[...] = middle
-    line_ref[...] = tally
+    middle_ref[0:256, :] = middle
+    middle_ref[256:264, :] = tally[:, 0:128]
+    middle_ref[264:272, :] = tally[:, 128:256]
     copy.wait()
     line = in_line(parent2_ref, 0, 2)
     third = iota((256, 256), 0)
@@ -140,13 +146,16 @@
             )
 
 
-def fine_kernel(rows_ref, ids_ref, acc_ref, wide_ref):
+def fine_kernel(rows_ref, out_ref, ids_ref, wide_ref, acc_ref):
     lane = iota((128, 128), 1)
     left = lane < PART
     half = jnp.where(left, 0.0, 1.0)
     group = lane >> 5
     down = iota((128, 128), 0)
+    for s in range(GROUPS):
+        ids_ref[8 * s : 8 * s + 8, :] = rows_ref[s, 128:144, :].astype(F32)[0:8]
     columns = jnp.transpose(ids_ref[...])
+    out_ref[:, 2176:2304] = columns
     for s in range(GROUPS):
         x = rows_ref[s, 0:128, :].astype(F32)
         y = turned(x)
@@ -172,7 +181,12 @@
             within = ids_ref[8 * s + 2 + j : 8 * s + 3 + j, :].astype(I32) & 127
             ones.append(hot(down == within))
         part = dot(jnp.concatenate(ones, axis=1), wide_ref[...])
-        acc_ref[...] = part if s == 0 else acc_ref[...] + part
+        if s == 0:
+            acc_ref[...] = part
+        elif s < GROUPS - 1:
+            acc_ref[...] += part
+        else:
+            out_ref[:, 0:2176] = acc_ref[...] + part
 
 
 def share_kernel(got_ref, acc_hbm, out_ref, count_ref):
@@ -185,106 +199,121 @@
 
 
 def ready_kernel(
-    shrink_ref, acc_ref, ids_ref, line_ref, third_ref, parent2_ref, parent3_ref, inv_ref, count_ref,
-    lines_ref, hot_ref, third_inv_ref, top_inv_ref, middle_inv_ref, top_hot_ref, top_turn_ref, middle_turn_ref,
+    shrink_ref, acc_ref, middle_ref, third_ref, parent2_ref, parent3_ref, lines_ref, fine_cols_ref,
+    cols_ref, top_inv_ref, middle_turn_ref,
 ):
     weight_top = shrink_ref[0] * (TOTAL / TOP)
     weight_third = shrink_ref[1] * (TOTAL / THIRD)
     weight_middle = shrink_ref[2] * (TOTAL / 8192)
     weight_fine = shrink_ref[3]
-    left = iota((256, 128), 1) < PART
-    columns = jnp.transpose(ids_ref[...])
+    left = iota((TOP, 128), 1) < PART
     tail = acc_ref[:, 2048:2176]
     square = tail[:, 0:32] + tail[:, 32:64] + tail[:, 64:96]
     count = tail[:, 96:128]
     lines_ref[...] = jnp.transpose(
         jnp.concatenate([square, count, jnp.zeros((128, 64), F32)], axis=1)
     )
-    inverse = 1.0 / (count + weight_fine)
+    fine_cols_ref[...] = jnp.concatenate(
+        [1.0 / (count + weight_fine), count, jnp.zeros((128, 64), F32)], axis=1
+    )
     across = iota((128, 256), 1)
-    for h in range(GROUPS):
-        here = slice(128 * h, 128 * (h + 1))
-        pair = (slice(2 * h, 2 * h + 1), slice(2 * h + 1, 2 * h + 2))
-        inv_ref[:, here] = jnp.where(left[0:128], inverse[:, pair[0]], inverse[:, pair[1]])
-        count_ref[:, here] = jnp.where(left[0:128], count[:, pair[0]], count[:, pair[1]])
-        for b in range(2):
-            parent = columns[:, 8 * h + 4 + b : 8 * h + 5 + b].astype(I32)
-            hot_ref[256 * h + 128 * b : 256 * h + 128 * (b + 1), :] = hot(across == parent)
-    tally = line_ref[0:1, :]
-    lines = jnp.concatenate(
-        [
-            third_ref[...],
-            tally[:, 0:128],
-            tally[:, 128:256],
-            parent2_ref[...].astype(F32),
-            parent3_ref[...].astype(F32),
-            jnp.zeros((116, 128), F32),
-        ],
-        axis=0,
-    )
-    columns = jnp.transpose(lines)
-    first = jnp.concatenate([columns[:, 0:1], columns[:, 1:2]], axis=0)
-    second = jnp.concatenate([columns[:, 2:3], columns[:, 3:4]], axis=0)
-    counts = jnp.where(left, first, second)
-    third_inv_ref[...] = 1.0 / (counts + weight_third)
-    tally = jnp.concatenate([columns[:, 4:5], columns[:, 5:6]], axis=0)
-    middle_inv_ref[...] = jnp.broadcast_to(1.0 / (tally + weight_middle), (256, 128))
-    top_id = iota((TOP, 256), 0)
-    top_first = hot(top_id == in_line(parent3_ref, 0, 2))
-    top_second = hot(top_id == in_line(parent3_ref, 2, 2))
-    top_hot_ref[0:TOP, :] = top_first
-    top_hot_ref[TOP : 2 * TOP, :] = top_second
-    parts = jnp.concatenate(pieces(counts, 3), axis=1)
-    first = dot(top_first, parts)
-    second = dot(top_second, parts)
-    first = first[:, 0:128] + first[:, 128:256] + first[:, 256:384]
-    second = second[:, 0:128] + second[:, 128:256] + second[:, 256:384]
-    top = jnp.where(left[0:TOP], first, second)
-    top_inv_ref[...] = 1.0 / (top + turned(top) + weight_top)
-    parents = [columns[:, 6 + k : 7 + k].astype(I32) for k in range(6)]
+    third = third_ref[...]
+    parent3 = parent3_ref[...].astype(F32)
+    parent2 = parent2_ref[...].astype(F32)
+    columns = jnp.transpose(
+        jnp.concatenate(
+            [
+                1.0 / (third + weight_third),
+                1.0 / (middle_ref[256:257, :] + weight_middle),
+                1.0 / (middle_ref[264:265, :] + weight_middle),
+                parent3,
+                parent2,
+                jnp.zeros((116, 128), F32),
+            ],
+            axis=0,
+        )
+    )
+    cols_ref[...] = columns
+    top_id = iota((TOP, 512), 0)
+    ones = hot(top_id == in_line(parent3_ref, 0, 4))
+    line = jnp.concatenate([third[k : k + 1] for k in range(4)], axis=1)
+    line = jnp.broadcast_to(line, (8, 512))
+    count = jnp.zeros((TOP, 8), F32)
+    for part in pieces(line, 3):
+        count = count + dot_last(ones, part)
+    top_inv_ref[...] = jnp.broadcast_to(1.0 / (count[:, 0:1] + weight_top), (TOP, 128))
     for k in range(2):
+        parent = columns[:, 10 + k : 11 + k].astype(I32)
         for b in range(2):
             middle_turn_ref[256 * b + 128 * k : 256 * b + 128 * (k + 1), :] = hot(
-                across + 256 * b == parents[k]
+                across + 256 * b == parent
             )
-    for k in range(4):
-        top_turn_ref[128 * k : 128 * (k + 1), :] = hot(across[:, 0:128] == parents[2 + k])[:, 0:TOP]
 
 
 def down_kernel(
-    shrink_ref, dp_ref, got_ref, middle_ref, acc_ref, inv_ref, count_ref, lines_ref, hot_ref, third_inv_ref,
-    top_inv_ref, middle_inv_ref, top_hot_ref, top_turn_ref, middle_turn_ref, send_ref, third_ref, diff_ref,
+    shrink_ref, dp_ref, got_ref, middle_ref, acc_ref, parent3_ref, lines_ref, fine_cols_ref, cols_ref,
+    top_inv_ref, middle_turn_ref, send_ref, third_ref, diff_ref,
 ):
     left = iota((256, 128), 1) < PART
     weight_top = shrink_ref[0] * (TOTAL / TOP)
     weight_third = shrink_ref[1] * (TOTAL / THIRD)
     weight_middle = shrink_ref[2] * (TOTAL / 8192)
     weight_fine = shrink_ref[3]
+    cols = cols_ref[...]
+    top_id = iota((TOP, 256), 0)
+    top_hot = jnp.concatenate(
+        [hot(top_id == in_line(parent3_ref, 0, 2)), hot(top_id == in_line(parent3_ref, 2, 2))], axis=0
+    )
+    across = iota((128, TOP), 1)
+    top_turn = jnp.concatenate(
+        [hot(across == cols[:, 6 + k : 7 + k].astype(I32)) for k in range(4)], axis=0
+    )
     third_sums = got_ref[...].reshape(256, 128)
-    top = two(dot(top_hot_ref[...], side(third_sums, 2)))
+    top = two(dot(top_hot, side(third_sums, 2)))
     top = jnp.where(left[0:TOP], top[0:TOP], top[TOP : 2 * TOP])
     top = top + turned(top)
     center = jnp.sum(top, axis=0, keepdims=True) / TOTAL
     top_means = (top + weight_top * center) * top_inv_ref[...]
-    prior = two(dot(top_turn_ref[...], side(top_means, 2)))
+    prior = two(dot(top_turn, side(top_means, 2)))
     prior = jnp.where(left, prior[0:256], prior[256:512])
-    third_means = (third_sums + weight_third * prior) * third_inv_ref[...]
+    inverse = jnp.where(
+        left,
+        jnp.concatenate([cols[:, 0:1], cols[:, 1:2]], axis=0),
+        jnp.concatenate([cols[:, 2:3], cols[:, 3:4]], axis=0),
+    )
+    third_means = (third_sums + weight_third * prior) * inverse
     third_ref[...] = third_means
     prior = two(dot(middle_turn_ref[...], side(third_means, 2)))
     prior = jnp.where(left, prior[0:256], prior[256:512])
     prior = prior + turned(prior)
-    middle_means = (middle_ref[...] + weight_middle * prior) * middle_inv_ref[...]
+    inverse = jnp.concatenate([cols[:, 4:5], cols[:, 5:6]], axis=0)
+    middle_means = (middle_ref[0:256, :] + weight_middle * prior) * inverse
     parts = side(middle_means, 2)
     left = left[0:128]
+    fine_cols = fine_cols_ref[...]
+    lane = iota((128, 128), 1).astype(F32)
+    lanes = (lane.astype(BF), (lane + 128.0).astype(BF))
+    one, zero = jnp.array(1, BF), jnp.array(0, BF)
     for h in range(GROUPS):
         here = slice(128 * h, 128 * (h + 1))
-        found = two(dot(hot_ref[256 * h : 256 * (h + 1), :], parts))
+        ones = []
+        for b in range(2):
+            parent = acc_ref[:, 2180 + 8 * h + b : 2181 + 8 * h + b]
+            parent = jnp.broadcast_to(parent, (128, 128)).astype(BF)
+            ones.append(
+                jnp.concatenate([jnp.where(lane == parent, one, zero) for lane in lanes], axis=1)
+            )
+        found = two(dot(jnp.concatenate(ones, axis=0), parts))
         prior = jnp.where(left, found[0:128], found[128:256])
         sums = acc_ref[:, here]
-        fine = ((sums + weight_fine * prior) * inv_ref[:, here]).astype(BF)
+        inverse = jnp.where(left, fine_cols[:, 2 * h : 2 * h + 1], fine_cols[:, 2 * h + 1 : 2 * h + 2])
+        count = jnp.where(
+            left, fine_cols[:, 32 + 2 * h : 33 + 2 * h], fine_cols[:, 33 + 2 * h : 34 + 2 * h]
+        )
+        fine = ((sums + weight_fine * prior) * inverse).astype(BF)
         send_ref[h, 0:128, :] = fine
         fine = fine.astype(F32)
-        hi, lo = pieces(fine * (count_ref[:, here] * fine - 2.0 * sums), 2)
+        hi, lo = pieces(fine * (count * fine - 2.0 * sums), 2)
         diff_ref[:, here] = hi
         diff_ref[:, 2048 + 128 * h : 2048 + 128 * (h + 1)] = lo
     select = hot((iota((2048, 128), 0) >> 6) == iota((2048, 128), 1))
@@ -376,23 +405,23 @@
         ],
     )(rows, fine_assign.reshape(2, 128), parent1.reshape(2, 128))
     group_rows = exchange(send, "clus")
-    third, middle, line, ids = call(
+    third, middle = call(
         middle_kernel,
         32,
         [VMEM, ANY],
-        [((DP, 3, 4, 128), F32), ((256, 128), F32), ((8, 256), F32), ((128, 128), F32)],
+        [((DP, 3, 4, 128), F32), ((272, 128), F32)],
         [pltpu.VMEM((512, 2048), BF), pltpu.VMEM((2, 128), I32), DMA],
     )(group_rows, parent2)
     third = exchange(third, "dp")
     (sums,) = call(
         fine_kernel,
         32,
-        [VMEM, VMEM],
-        [((128, 2176), F32)],
-        [pltpu.VMEM((256, 2176), BF)],
+        [VMEM],
+        [((128, 2304), F32)],
+        [pltpu.VMEM((128, 128), F32), pltpu.VMEM((256, 2176), BF), pltpu.VMEM((128, 2176), F32)],
         4_000_000_000,
         4_000_000,
-    )(group_rows, ids)
+    )(group_rows)
     third, counts = call(
         share_kernel,
         16, [VMEM, ANY], [((DP, 8, 128), F32), ((4, 128), F32)]
@@ -400,38 +429,33 @@
     third = exchange(third, "dp")
     ready = call(
         ready_kernel,
-        60,
-        [SMEM] + [VMEM] * 6,
+        24,
+        [SMEM] + [VMEM] * 5,
         [
-            ((128, 2048), F32),
-            ((128, 2048), F32),
             ((128, 128), F32),
-            ((4096, 256), BF),
-            ((256, 128), F32),
+            ((128, 128), F32),
+            ((128, 128), F32),
             ((TOP, 128), F32),
-            ((256, 128), F32),
-            ((2 * TOP, 256), BF),
-            ((THIRD, TOP), BF),
             ((2 * MIDDLE, 256), BF),
         ],
         (),
         1_000_000_000,
         8_000_000,
-    )(shrink, sums, ids, line, counts, parent2, parent3)
+    )(shrink, sums, middle, counts, parent2, parent3)
     (send,) = call(
         down_kernel,
-        59,
-        [SMEM, SMEM] + [VMEM] * 13,
+        24,
+        [SMEM, SMEM] + [VMEM] * 9,
         [block],
         [pltpu.VMEM((256, 128), F32), pltpu.VMEM((128, 4096), BF)],
-    )(shrink, dp, third, middle, sums, *ready)
+    )(shrink, dp, third, middle, sums, parent3, *ready)
     got = exchange(send, "clus")
     fine, middle, third, spread = call(
         finish_kernel,
         16,
         [SMEM, VMEM, VMEM],
         [((256, 1024), BF), ((16, 1024), BF), ((1, 1024), BF), ((2, 128), F32)],
-    )(clus, got, ready[2])
+    )(clus, got, ready[0])
     return fine, middle, third, spread.reshape(256)
 
 

time: 105 us -> 101 us (0.962)
  the two profiles are of different devices: /device:TPU:10 before, /device:TPU:8 now
where the time goes in v3:
time: 101 us; the launch traced here: 100 us
  waiting for transfers between devices  32.8 us (32%)
  blocking collectives  26.5 us (26%)
  starting transfers between devices  21.9 us (22%)
  Pallas kernels  18.4 us (18%)
    all_to_all x3, waiting for transfers between devices, exchange(): return lax.all_to_all(x, axis, split_axis=0, concat_axis=0, tiled=True)  32.8 us
    all_to_all x1, blocking collectives, exchange(): return lax.all_to_all(x, axis, split_axis=0, concat_axis=0, tiled=True)  26.5 us
    all_to_all x3, starting transfers between devices, exchange(): return lax.all_to_all(x, axis, split_axis=0, concat_axis=0, tiled=True)  21.9 us
    pallas_call x1, Pallas kernels, local(): call(fine_kernel, 32, [VMEM], [((128, 2304), F32)], [pltpu.VMEM((128, 128...  6.6 us
    pallas_call x1, Pallas kernels, local(): call(down_kernel, 24, [SMEM, SMEM] + [VMEM] * 9, [block], [pltpu.VMEM((25...  4.29 us
    pallas_call x1, Pallas kernels, local(): call(middle_kernel, 32, [VMEM, ANY], [((DP, 3, 4, 128), F32), ((272, 128)...  2.72 us
    pallas_call x1, Pallas kernels, local(): call(pack_kernel, 60, [ANY] * 3, [block], [pltpu.VMEM((256, WIDTH), BF),...  2.11 us
  transfers between devices with their start and end apart: 3, of which 3 were waited for; matrix products, arithmetic and copies ran while one was open for 0% of the time, Pallas kernels for 7%

profile of v3, /device:TPU:8, one launch (start us, length us, event | category | flops | bytes accessed | tf_op | source)
XLA Modules:
  0.0 100.3 jit_solution(11264584234136134628)
XLA Ops:
  0.6 0.0 copy-start.1
  0.6 2.1 %shard_map.93 = bf16[16,144,128]{2,1,0:T(8,128)(2,1)} custom-call(bf16[256,1024]{1,0:T(8,128)(2,1)} %rows_hbm.1, s32[2,128]{1,0:T(2,128)} %bitcast.11, s32[2,128]{1,0:T(2,128)} %bitcast.12), custom_call_target="tpu_custom_call" | custom-call | tf_op jit(solution)/shard_map/pallas_call | solution.py:395
  2.8 26.5 %all_to_all.20.rows_ref = bf16[16,144,128]{2,1,0:T(8,128)(2,1)S(1)} all-to-all(bf16[16,144,128]{2,1,0:T(8,128)(2,1)} %shard_map.93), channel_id=1, replica_groups=mesh['dp'=32,'clus'=16] {'clus'}, dimensions={0} | all-to-all | bytes 1179648 | tf_op jit(solution)/shard_map/all_to_all | solution.py:386
  29.3 0.0 copy-done.1
  29.3 2.7 %shard_map.94 = (f32[32,3,4,128]{3,2,1,0:T(4,128)}, f32[272,128]{1,0:T(8,128)S(1)}) custom-call(bf16[16,144,128]{2,1,0:T(8,128)(2,1)S(1)} %all_to_all.20.rows_ref, s32[2,128]{1,0:T(2,128)S(1)} %bitcast.9), custom_call_target="tpu_custom_call" | custom-call | tf_op jit(solution)/shard_map/pallas_call | solution.py:408
  32.0 12.9 %all-to-all-start.1 = ((f32[32,3,4,128]{3,2,1,0:T(4,128)}), f32[32,3,4,128]{3,2,1,0:T(4,128)S(1)}, u32[]{:S(2)}, u32[]{:S(2)}) async-start(f32[32,3,4,128]{3,2,1,0:T(4,128)} %get-tuple-element.17), calls=%async_computation.1 | async-start | bytes 393216 | tf_op jit(solution)/shard_map/all_to_all | solution.py:386
  44.9 6.6 %shard_map.95.acc_hbm.acc_ref = f32[128,2304]{1,0:T(8,128)S(1)} custom-call(bf16[16,144,128]{2,1,0:T(8,128)(2,1)S(1)} %all_to_all.20.rows_ref), custom_call_target="tpu_custom_call" | custom-call | flops 4000000000 | bytes 4000000 | tf_op jit(solution)/shard_map/pallas_call | solution.py:416
  51.5 0.0 copy-start
  51.5 0.0 copy-start.2
  51.5 5.4 %all-to-all-done.1.got_ref = f32[32,3,4,128]{3,2,1,0:T(4,128)S(1)} async-done(((f32[32,3,4,128]{3,2,1,0:T(4,128)}), f32[32,3,4,128]{3,2,1,0:T(4,128)S(1)}, u32[]{:S(2)}, u32[]{:S(2)}) %all-to-all-start.1) | async-done | bytes 196640 | tf_op jit(solution)/shard_map/all_to_all | solution.py:386
  56.9 0.7 shard_map.96
  57.6 4.4 %all-to-all-start.2 = ((f32[32,8,128]{2,1,0:T(8,128)}), f32[32,8,128]{2,1,0:T(8,128)S(1)}, u32[]{:S(2)}, u32[]{:S(2)}) async-start(f32[32,8,128]{2,1,0:T(8,128)} %get-tuple-element.18), calls=%async_computation.2 | async-start | bytes 262144 | tf_op jit(solution)/shard_map/all_to_all | solution.py:386
  62.0 0.0 copy-done
  62.1 0.0 copy-done.2
  62.1 0.9 shard_map.97
  63.0 9.8 %all-to-all-done.2.got_ref = f32[32,8,128]{2,1,0:T(8,128)S(1)} async-done(((f32[32,8,128]{2,1,0:T(8,128)}), f32[32,8,128]{2,1,0:T(8,128)S(1)}, u32[]{:S(2)}, u32[]{:S(2)}) %all-to-all-start.2) | async-done | bytes 131104 | tf_op jit(solution)/shard_map/all_to_all | solution.py:386
  72.8 4.3 %shard_map.98 = bf16[16,144,128]{2,1,0:T(8,128)(2,1)} custom-call(f32[4]{0:T(128)S(1)} %copy-done.2, s32[1]{0:T(128)} %bitcast.1.dp_ref, f32[32,8,128]{2,1,0:T(8,128)S(1)} %all-to-all-done.2.got_ref, f32[272,128]{1,0:T(8,128)S(1)} %get-tuple-element.19.middle_ref, f32[128,2304]{1,0:T(8,128)S(1)} %shard_map.95.acc_hbm.acc_ref, s32[4,128]{1,0:T(4,128)S(1)} %bitcast.8, ...), custom_call_target="tpu_custom_call" | custom-call | tf_op jit(solution)/shard_map/pallas_call | solution.py:445
  77.1 4.6 %all-to-all-start.3 = ((bf16[16,144,128]{2,1,0:T(8,128)(2,1)}), bf16[16,144,128]{2,1,0:T(8,128)(2,1)S(1)}, u32[]{:S(2)}, u32[]{:S(2)}) async-start(bf16[16,144,128]{2,1,0:T(8,128)(2,1)} %shard_map.98), calls=%async_computation.3 | async-start | bytes 1179648 | tf_op jit(solution)/shard_map/all_to_all | solution.py:386
  81.7 17.5 %all-to-all-done.3.got_ref = bf16[16,144,128]{2,1,0:T(8,128)(2,1)S(1)} async-done(((bf16[16,144,128]{2,1,0:T(8,128)(2,1)}), bf16[16,144,128]{2,1,0:T(8,128)(2,1)S(1)}, u32[]{:S(2)}, u32[]{:S(2)}) %all-to-all-start.3) | async-done | bytes 589856 | tf_op jit(solution)/shard_map/all_to_all | solution.py:386
  99.2 1.1 %shard_map.99 = (bf16[256,1024]{1,0:T(8,128)(2,1)}, bf16[16,1024]{1,0:T(8,128)(2,1)}, bf16[1,1024]{1,0:T(2,128)(2,1)}, f32[2,128]{1,0:T(2,128)}) custom-call(s32[1]{0:T(128)} %bitcast.clus_ref, bf16[16,144,128]{2,1,0:T(8,128)(2,1)S(1)} %all-to-all-done.3.got_ref, f32[128,128]{1,0:T(8,128)S(1)} %get-tuple-element.21.lines_ref), custom_call_target="tpu_custom_call" | custom-call | tf_op jit(solution)/shard_map/pallas_call | solution.py:453
Async XLA Ops:
  0.6 28.7 %copy-start.1 = (s32[256]{0:T(256)S(1)}, s32[256]{0:T(256)}, u32[]{:S(2)}) copy-start(s32[256]{0:T(256)} %param.9) | copy-start | bytes 3076
  32.0 24.9 %all-to-all-start.1 = ((f32[32,3,4,128]{3,2,1,0:T(4,128)}), f32[32,3,4,128]{3,2,1,0:T(4,128)S(1)}, u32[]{:S(2)}, u32[]{:S(2)}) async-start(f32[32,3,4,128]{3,2,1,0:T(4,128)} %get-tuple-element.17), calls=%async_computation.1 | async-start | bytes 393216 | tf_op jit(solution)/shard_map/all_to_all | solution.py:386
  51.5 10.5 %copy-start = (s32[512]{0:T(512)S(1)}, s32[512]{0:T(512)}, u32[]{:S(2)}) copy-start(s32[512]{0:T(512)} %param.10) | copy-start | bytes 6148
  51.5 10.5 %copy-start.2 = (f32[4]{0:T(128)S(1)}, f32[4]{0:T(128)}, u32[]{:S(2)}) copy-start(f32[4]{0:T(128)} %shrink_ref.3) | copy-start | bytes 52
  57.6 15.2 %all-to-all-start.2 = ((f32[32,8,128]{2,1,0:T(8,128)}), f32[32,8,128]{2,1,0:T(8,128)S(1)}, u32[]{:S(2)}, u32[]{:S(2)}) async-start(f32[32,8,128]{2,1,0:T(8,128)} %get-tuple-element.18), calls=%async_computation.2 | async-start | bytes 262144 | tf_op jit(solution)/shard_map/all_to_all | solution.py:386
  77.1 22.1 %all-to-all-start.3 = ((bf16[16,144,128]{2,1,0:T(8,128)(2,1)}), bf16[16,144,128]{2,1,0:T(8,128)(2,1)S(1)}, u32[]{:S(2)}, u32[]{:S(2)}) async-start(bf16[16,144,128]{2,1,0:T(8,128)(2,1)} %shard_map.98), calls=%async_computation.3 | async-start | bytes 1179648 | tf_op jit(solution)/shard_map/all_to_all | solution.py:386

commit v4 on v3

--- a/solution.py
+++ b/solution.py
@@ -69,17 +69,7 @@
     return jnp.concatenate([ref[first + k : first + k + 1, :] for k in range(count)], axis=1)
 
 
-def pack_kernel(rows_hbm, assign_hbm, parent1_hbm, send_ref, rows_ref, assign_ref, parent1_ref, sems):
-    copies = [
-        pltpu.make_async_copy(src, dst, sems.at[k])
-        for k, (src, dst) in enumerate(
-            [(rows_hbm, rows_ref), (assign_hbm, assign_ref), (parent1_hbm, parent1_ref)]
-        )
-    ]
-    for copy in copies:
-        copy.start()
-    copies[1].wait()
-    copies[2].wait()
+def pack_kernel(rows_ref, assign_ref, parent1_ref, send_ref):
     fine = assign_ref[...] & (GROUPS * FINE - 1)
     parent = parent1_ref[...] & (MIDDLE - 1)
     tile = jnp.concatenate(
@@ -91,15 +81,14 @@
         ],
         axis=0,
     ).astype(BF)
-    for k in range(GROUPS):
-        send_ref[k, 128:144, :] = tile
-    copies[0].wait()
     left = iota((128, 128), 1) < PART
     for g in range(GROUPS // 2):
         top = rows_ref[0:128, 128 * g : 128 * (g + 1)].astype(F32)
         low = rows_ref[128:256, 128 * g : 128 * (g + 1)].astype(F32)
         send_ref[2 * g, 0:128, :] = jnp.where(left, top, turned(low)).astype(BF)
         send_ref[2 * g + 1, 0:128, :] = jnp.where(left, turned(top), low).astype(BF)
+        send_ref[2 * g, 128:144, :] = tile
+        send_ref[2 * g + 1, 128:144, :] = tile
 
 
 def middle_kernel(rows_ref, parent2_hbm, third_ref, middle_ref, hot_ref, parent2_ref, sem):
@@ -199,60 +188,79 @@
 
 
 def ready_kernel(
-    shrink_ref, acc_ref, middle_ref, third_ref, parent2_ref, parent3_ref, lines_ref, fine_cols_ref,
-    cols_ref, top_inv_ref, middle_turn_ref,
+    index_ref, shrink_ref, acc_ref, middle_ref, third_ref, parent2_ref, parent3_ref, inv_ref, lines_ref, cols_ref,
+    middle_turn_ref, top_turn_ref, third_inv_ref, top_inv_ref, down_ref, scale_ref, own_ref,
 ):
-    weight_top = shrink_ref[0] * (TOTAL / TOP)
     weight_third = shrink_ref[1] * (TOTAL / THIRD)
     weight_middle = shrink_ref[2] * (TOTAL / 8192)
-    weight_fine = shrink_ref[3]
-    left = iota((TOP, 128), 1) < PART
+    left = iota((128, 128), 1) < PART
     tail = acc_ref[:, 2048:2176]
     square = tail[:, 0:32] + tail[:, 32:64] + tail[:, 64:96]
     count = tail[:, 96:128]
-    lines_ref[...] = jnp.transpose(
-        jnp.concatenate([square, count, jnp.zeros((128, 64), F32)], axis=1)
-    )
-    fine_cols_ref[...] = jnp.concatenate(
-        [1.0 / (count + weight_fine), count, jnp.zeros((128, 64), F32)], axis=1
-    )
-    across = iota((128, 256), 1)
+    lines = jnp.transpose(jnp.concatenate([square, count, jnp.zeros((128, 64), F32)], axis=1))
+    lines_ref[...] = lines[0:64]
+    row = iota((32, 128), 0)
+    own = [
+        jnp.sum(jnp.where(row == 2 * index_ref[1] + b, lines[32:64], 0.0), axis=0, keepdims=True)
+        for b in range(2)
+    ]
+    own_ref[...] = jnp.concatenate(own + [jnp.zeros((6, 128), F32)], axis=0)
+    inverse = 1.0 / (count + shrink_ref[3])
+    for h in range(GROUPS):
+        inv_ref[:, 128 * h : 128 * (h + 1)] = jnp.where(
+            left, inverse[:, 2 * h : 2 * h + 1], inverse[:, 2 * h + 1 : 2 * h + 2]
+        )
     third = third_ref[...]
-    parent3 = parent3_ref[...].astype(F32)
-    parent2 = parent2_ref[...].astype(F32)
-    columns = jnp.transpose(
+    cols = jnp.transpose(
         jnp.concatenate(
             [
-                1.0 / (third + weight_third),
                 1.0 / (middle_ref[256:257, :] + weight_middle),
                 1.0 / (middle_ref[264:265, :] + weight_middle),
-                parent3,
-                parent2,
+                parent3_ref[...].astype(F32),
+                parent2_ref[...].astype(F32),
+                1.0 / (third + weight_third),
                 jnp.zeros((116, 128), F32),
             ],
             axis=0,
         )
     )
-    cols_ref[...] = columns
-    top_id = iota((TOP, 512), 0)
-    ones = hot(top_id == in_line(parent3_ref, 0, 4))
-    line = jnp.concatenate([third[k : k + 1] for k in range(4)], axis=1)
-    line = jnp.broadcast_to(line, (8, 512))
-    count = jnp.zeros((TOP, 8), F32)
-    for part in pieces(line, 3):
-        count = count + dot_last(ones, part)
-    top_inv_ref[...] = jnp.broadcast_to(1.0 / (count[:, 0:1] + weight_top), (TOP, 128))
+    third_inv_ref[...] = jnp.concatenate(
+        [jnp.where(left, cols[:, 8 + k : 9 + k], cols[:, 10 + k : 11 + k]) for k in range(2)], axis=0
+    )
+    across = iota((128, 256), 1)
     for k in range(2):
-        parent = columns[:, 10 + k : 11 + k].astype(I32)
+        parent = cols[:, 6 + k : 7 + k].astype(I32)
         for b in range(2):
             middle_turn_ref[256 * b + 128 * k : 256 * b + 128 * (k + 1), :] = hot(
                 across + 256 * b == parent
             )
+    for k in range(4):
+        top_turn_ref[128 * k : 128 * (k + 1), :] = hot(
+            across[:, 0:128] == cols[:, 2 + k : 3 + k].astype(I32)
+        )
+    down = jnp.zeros((256, 128), F32)
+    scale = jnp.zeros((256, 128), F32)
+    for b in range(2):
+        turn = middle_turn_ref[256 * b : 256 * (b + 1), :]
+        down = down + dot(turn, top_turn_ref[256 * b : 256 * (b + 1), :])
+        column = jnp.concatenate([cols[:, 8 + 2 * b + k : 9 + 2 * b + k] for k in range(2)], axis=0)
+        for part in pieces(jnp.broadcast_to(weight_third * column, (256, 128)), 3):
+            scale = scale + dot(turn, part)
+    down_ref[...] = down.astype(BF)
+    scale_ref[...] = scale
+    ones = hot(iota((TOP, 512), 0) == in_line(parent3_ref, 0, 4))
+    line = jnp.concatenate([third[k : k + 1] for k in range(4)], axis=1)
+    parts = pieces(jnp.broadcast_to(line, (8, 512)), 3)
+    count = dot_last(ones, parts[0]) + dot_last(ones, parts[1]) + dot_last(ones, parts[2])
+    top_inv_ref[...] = jnp.broadcast_to(
+        1.0 / (count[:, 0:1] + shrink_ref[0] * (TOTAL / TOP)), (TOP, 128)
+    )
+    cols_ref[...] = cols
 
 
 def down_kernel(
-    shrink_ref, dp_ref, got_ref, middle_ref, acc_ref, parent3_ref, lines_ref, fine_cols_ref, cols_ref,
-    top_inv_ref, middle_turn_ref, send_ref, third_ref, diff_ref,
+    index_ref, shrink_ref, got_ref, middle_ref, parent3_ref, acc_ref, inv_ref, lines_ref, cols_ref, middle_turn_ref,
+    top_turn_ref, third_inv_ref, top_inv_ref, down_ref, scale_ref, send_ref,
 ):
     left = iota((256, 128), 1) < PART
     weight_top = shrink_ref[0] * (TOTAL / TOP)
@@ -264,36 +272,29 @@
     top_hot = jnp.concatenate(
         [hot(top_id == in_line(parent3_ref, 0, 2)), hot(top_id == in_line(parent3_ref, 2, 2))], axis=0
     )
-    across = iota((128, TOP), 1)
-    top_turn = jnp.concatenate(
-        [hot(across == cols[:, 6 + k : 7 + k].astype(I32)) for k in range(4)], axis=0
-    )
     third_sums = got_ref[...].reshape(256, 128)
     top = two(dot(top_hot, side(third_sums, 2)))
     top = jnp.where(left[0:TOP], top[0:TOP], top[TOP : 2 * TOP])
     top = top + turned(top)
     center = jnp.sum(top, axis=0, keepdims=True) / TOTAL
     top_means = (top + weight_top * center) * top_inv_ref[...]
-    prior = two(dot(top_turn, side(top_means, 2)))
-    prior = jnp.where(left, prior[0:256], prior[256:512])
-    inverse = jnp.where(
-        left,
-        jnp.concatenate([cols[:, 0:1], cols[:, 1:2]], axis=0),
-        jnp.concatenate([cols[:, 2:3], cols[:, 3:4]], axis=0),
-    )
-    third_means = (third_sums + weight_third * prior) * inverse
-    third_ref[...] = third_means
-    prior = two(dot(middle_turn_ref[...], side(third_means, 2)))
-    prior = jnp.where(left, prior[0:256], prior[256:512])
-    prior = prior + turned(prior)
-    inverse = jnp.concatenate([cols[:, 4:5], cols[:, 5:6]], axis=0)
+    term = two(dot(middle_turn_ref[...], side(third_sums * third_inv_ref[...], 2)))
+    term = jnp.where(left, term[0:256], term[256:512])
+    parts = side(top_means, 2)
+    prior = term + turned(term) + scale_ref[...] * two(dot(down_ref[:, 0:TOP], parts))
+    index = index_ref[0]
+    rows = pl.ds(pl.multiple_of((index % 16) * 16, 16), 16)
+    own = two(dot(top_turn_ref[pl.ds(pl.multiple_of(index * 16, 16), 16), 0:TOP], parts))
+    own = (got_ref[pl.ds((index % 16) * 2, 2)].reshape(16, 128) + weight_third * own) * third_inv_ref[rows, :]
+    own = jnp.where(index < 16, own, turned(own))
+    inverse = jnp.concatenate([cols[:, 0:1], cols[:, 1:2]], axis=0)
     middle_means = (middle_ref[0:256, :] + weight_middle * prior) * inverse
     parts = side(middle_means, 2)
     left = left[0:128]
-    fine_cols = fine_cols_ref[...]
     lane = iota((128, 128), 1).astype(F32)
     lanes = (lane.astype(BF), (lane + 128.0).astype(BF))
     one, zero = jnp.array(1, BF), jnp.array(0, BF)
+    halves = hot((iota((16, 256), 1) & 127) >> 6 == iota((16, 256), 0))
     for h in range(GROUPS):
         here = slice(128 * h, 128 * (h + 1))
         ones = []
@@ -306,40 +307,28 @@
         found = two(dot(jnp.concatenate(ones, axis=0), parts))
         prior = jnp.where(left, found[0:128], found[128:256])
         sums = acc_ref[:, here]
-        inverse = jnp.where(left, fine_cols[:, 2 * h : 2 * h + 1], fine_cols[:, 2 * h + 1 : 2 * h + 2])
-        count = jnp.where(
-            left, fine_cols[:, 32 + 2 * h : 33 + 2 * h], fine_cols[:, 33 + 2 * h : 34 + 2 * h]
-        )
-        fine = ((sums + weight_fine * prior) * inverse).astype(BF)
+        fine = ((sums + weight_fine * prior) * inv_ref[:, here]).astype(BF)
         send_ref[h, 0:128, :] = fine
         fine = fine.astype(F32)
-        hi, lo = pieces(fine * (count * fine - 2.0 * sums), 2)
-        diff_ref[:, here] = hi
-        diff_ref[:, 2048 + 128 * h : 2048 + 128 * (h + 1)] = lo
-    select = hot((iota((2048, 128), 0) >> 6) == iota((2048, 128), 1))
-    diff = dot(diff_ref[:, 0:2048], select) + dot(diff_ref[:, 2048:4096], select)
-    spread = jnp.transpose(diff)[0:32] + lines_ref[0:32]
-    spread = [p.astype(F32) for p in pieces(spread, 3)]
-    dp = dp_ref[0]
-    own = third_ref[pl.ds(pl.multiple_of((dp % 16) * 16, 16), 16), :]
-    own = jnp.where(dp < 16, own, turned(own))
-    for h in range(GROUPS):
+        spread = (
+            lines_ref[2 * h : 2 * h + 2]
+            + lines_ref[32 + 2 * h : 34 + 2 * h] * dot_last(halves, side(fine * fine, 2))[0:2]
+            - 2.0 * dot_last(halves, side(fine * sums, 2))[0:2]
+        )
         send_ref[h, 128:144, :] = jnp.concatenate(
             [
                 jnp.where(
                     left[0:8], middle_means[16 * h : 16 * h + 8], middle_means[16 * h + 8 : 16 * h + 16]
                 ),
                 own[h : h + 1],
-                spread[0][2 * h : 2 * h + 2],
-                spread[1][2 * h : 2 * h + 2],
-                spread[2][2 * h : 2 * h + 2],
-                jnp.zeros((1, 128), F32),
-            ],
+            ]
+            + [part.astype(F32) for part in pieces(spread, 3)]
+            + [jnp.zeros((1, 128), F32)],
             axis=0,
         ).astype(BF)
 
 
-def finish_kernel(clus_ref, got_ref, lines_ref, out_ref, middle_ref, third_ref, spread_ref):
+def finish_kernel(got_ref, own_ref, out_ref, middle_ref, third_ref, spread_ref):
     left = iota((128, 128), 1) < PART
     total = jnp.zeros((8, 128), F32)
     for g in range(GROUPS // 2):
@@ -356,12 +345,7 @@
         third_ref[:, here] = first[8:9].astype(BF)
         total = total + a[8:16] + b[8:16]
     total = total[1:3] + total[3:5] + total[5:7]
-    row = iota((32, 128), 0)
-    counts = [
-        jnp.sum(jnp.where(row == 2 * clus_ref[0] + b, lines_ref[32:64], 0.0), axis=0, keepdims=True)
-        for b in range(2)
-    ]
-    spread_ref[...] = total / (WIDTH * (jnp.concatenate(counts, axis=0) + 1.0))
+    spread_ref[...] = total / (WIDTH * (own_ref[0:2] + 1.0))
 
 
 VMEM = pl.BlockSpec(memory_space=pltpu.VMEM)
@@ -387,27 +371,17 @@
 
 
 def local(rows, fine_assign, parent1, parent2, parent3, shrink):
-    dp = lax.axis_index("dp").astype(I32).reshape(1)
-    clus = lax.axis_index("clus").astype(I32).reshape(1)
+    index = jnp.stack([lax.axis_index("dp"), lax.axis_index("clus")]).astype(I32)
     parent2 = parent2.reshape(2, 128)
     parent3 = parent3.reshape(4, 128)
     block = ((GROUPS, ROWS, 128), BF)
-    (send,) = call(
-        pack_kernel,
-        60,
-        [ANY] * 3,
-        [block],
-        [
-            pltpu.VMEM((256, WIDTH), BF),
-            pltpu.VMEM((2, 128), I32),
-            pltpu.VMEM((2, 128), I32),
-            DMA((3,)),
-        ],
-    )(rows, fine_assign.reshape(2, 128), parent1.reshape(2, 128))
+    (send,) = call(pack_kernel, 60, [VMEM] * 3, [block])(
+        rows, fine_assign.reshape(2, 128), parent1.reshape(2, 128)
+    )
     group_rows = exchange(send, "clus")
     third, middle = call(
         middle_kernel,
-        32,
+        24,
         [VMEM, ANY],
         [((DP, 3, 4, 128), F32), ((272, 128), F32)],
         [pltpu.VMEM((512, 2048), BF), pltpu.VMEM((2, 128), I32), DMA],
@@ -415,47 +389,45 @@
     third = exchange(third, "dp")
     (sums,) = call(
         fine_kernel,
-        32,
+        24,
         [VMEM],
         [((128, 2304), F32)],
         [pltpu.VMEM((128, 128), F32), pltpu.VMEM((256, 2176), BF), pltpu.VMEM((128, 2176), F32)],
         4_000_000_000,
         4_000_000,
     )(group_rows)
-    third, counts = call(
-        share_kernel,
-        16, [VMEM, ANY], [((DP, 8, 128), F32), ((4, 128), F32)]
-    )(third, sums)
+    third, counts = call(share_kernel, 24, [VMEM, ANY], [((DP, 8, 128), F32), ((4, 128), F32)])(
+        third, sums
+    )
     third = exchange(third, "dp")
-    ready = call(
+    *ready, own = call(
         ready_kernel,
         24,
-        [SMEM] + [VMEM] * 5,
+        [SMEM, SMEM] + [VMEM] * 5,
         [
+            ((128, 2048), F32),
+            ((64, 128), F32),
             ((128, 128), F32),
-            ((128, 128), F32),
-            ((128, 128), F32),
+            ((2 * MIDDLE, 256), BF),
+            ((THIRD, 128), BF),
+            ((256, 128), F32),
             ((TOP, 128), F32),
-            ((2 * MIDDLE, 256), BF),
+            ((256, 128), BF),
+            ((256, 128), F32),
+            ((8, 128), F32),
         ],
         (),
         1_000_000_000,
         8_000_000,
-    )(shrink, sums, middle, counts, parent2, parent3)
-    (send,) = call(
-        down_kernel,
-        24,
-        [SMEM, SMEM] + [VMEM] * 9,
-        [block],
-        [pltpu.VMEM((256, 128), F32), pltpu.VMEM((128, 4096), BF)],
-    )(shrink, dp, third, middle, sums, parent3, *ready)
+    )(index, shrink, sums, middle, counts, parent2, parent3)
+    (send,) = call(down_kernel, 24, [SMEM, SMEM] + [VMEM] * 13, [block])(index, shrink, third, middle, parent3, sums, *ready)
     got = exchange(send, "clus")
     fine, middle, third, spread = call(
         finish_kernel,
-        16,
-        [SMEM, VMEM, VMEM],
+        24,
+        [VMEM, VMEM],
         [((256, 1024), BF), ((16, 1024), BF), ((1, 1024), BF), ((2, 128), F32)],
-    )(clus, got, ready[0])
+    )(got, own)
     return fine, middle, third, spread.reshape(256)
 
 

time: 101 us -> 99.1 us (0.981)
  blocking collectives: 26.5 us -> 49 us
  waiting for transfers between devices: 32.8 us -> 14.1 us
  starting transfers between devices: 21.9 us -> 17.3 us
    all_to_all x1 -> x2, blocking collectives: 26.5 us -> 49 us  [exchange(): return lax.all_to_all(x, axis, split_axis=0, concat_axis=0, tiled=True)]
    all_to_all x3 -> x2, waiting for transfers between devices: 32.8 us -> 14.1 us  [exchange(): return lax.all_to_all(x, axis, split_axis=0, concat_axis=0, tiled=True)]
    all_to_all x3 -> x2, starting transfers between devices: 21.9 us -> 17.3 us  [exchange(): return lax.all_to_all(x, axis, split_axis=0, concat_axis=0, tiled=True)]
  transfers between devices with their start and end apart: 3 -> 2, of which waited for: 3 -> 2; matrix products, arithmetic and copies ran while one was open for 0% -> 0% of each run, Pallas kernels for 7% -> 9%
where the time goes in v4:
time: 99.1 us; the launch traced here: 98.7 us
  blocking collectives  49 us (49%)
  Pallas kernels  17.5 us (18%)
  starting transfers between devices  17.3 us (17%)
  waiting for transfers between devices  14.1 us (14%)
    all_to_all x2, blocking collectives, exchange(): return lax.all_to_all(x, axis, split_axis=0, concat_axis=0, tiled=True)  49 us
    all_to_all x2, starting transfers between devices, exchange(): return lax.all_to_all(x, axis, split_axis=0, concat_axis=0, tiled=True)  17.3 us
    all_to_all x2, waiting for transfers between devices, exchange(): return lax.all_to_all(x, axis, split_axis=0, concat_axis=0, tiled=True)  14.1 us
    pallas_call x1, Pallas kernels, local(): call(fine_kernel, 24, [VMEM], [((128, 2304), F32)], [pltpu.VMEM((128, 128...  6.58 us
    pallas_call x1, Pallas kernels, local(): call(middle_kernel, 24, [VMEM, ANY], [((DP, 3, 4, 128), F32), ((272, 128)...  2.72 us
    pallas_call x1, Pallas kernels, local(): call(down_kernel, 24, [SMEM, SMEM] + [VMEM] * 13, [block])  2.4 us
    pallas_call x1, Pallas kernels, local(): call(pack_kernel, 60, [VMEM] * 3, [block])  2.11 us
  transfers between devices with their start and end apart: 2, of which 2 were waited for; matrix products, arithmetic and copies ran while one was open for 0% of the time, Pallas kernels for 9%

profile of v4, /device:TPU:8, one launch (start us, length us, event | category | flops | bytes accessed | tf_op | source)
XLA Modules:
  0.0 98.7 jit_solution(7138461250696871746)
XLA Ops:
  0.6 0.0 copy-start.1
  0.6 2.1 %shard_map.93 = bf16[16,144,128]{2,1,0:T(8,128)(2,1)} custom-call(bf16[256,1024]{1,0:T(8,128)(2,1)} %rows_ref.1, s32[2,128]{1,0:T(2,128)} %bitcast.11, s32[2,128]{1,0:T(2,128)} %bitcast.12), custom_call_target="tpu_custom_call" | custom-call | tf_op jit(solution)/shard_map/pallas_call | solution.py:378
  2.8 26.5 %all_to_all.20.rows_ref = bf16[16,144,128]{2,1,0:T(8,128)(2,1)S(1)} all-to-all(bf16[16,144,128]{2,1,0:T(8,128)(2,1)} %shard_map.93), channel_id=1, replica_groups=mesh['dp'=32,'clus'=16] {'clus'}, dimensions={0} | all-to-all | bytes 1179648 | tf_op jit(solution)/shard_map/all_to_all | solution.py:370
  29.3 0.0 copy-done.1
  29.3 2.7 %shard_map.94 = (f32[32,3,4,128]{3,2,1,0:T(4,128)}, f32[272,128]{1,0:T(8,128)S(1)}) custom-call(bf16[16,144,128]{2,1,0:T(8,128)(2,1)S(1)} %all_to_all.20.rows_ref, s32[2,128]{1,0:T(2,128)S(1)} %bitcast.9), custom_call_target="tpu_custom_call" | custom-call | tf_op jit(solution)/shard_map/pallas_call | solution.py:382
  32.0 12.9 %all-to-all-start.1 = ((f32[32,3,4,128]{3,2,1,0:T(4,128)}), f32[32,3,4,128]{3,2,1,0:T(4,128)S(1)}, u32[]{:S(2)}, u32[]{:S(2)}) async-start(f32[32,3,4,128]{3,2,1,0:T(4,128)} %get-tuple-element.22), calls=%async_computation.1 | async-start | bytes 393216 | tf_op jit(solution)/shard_map/all_to_all | solution.py:370
  44.9 6.6 %shard_map.95.acc_hbm.acc_ref = f32[128,2304]{1,0:T(8,128)S(1)} custom-call(bf16[16,144,128]{2,1,0:T(8,128)(2,1)S(1)} %all_to_all.20.rows_ref), custom_call_target="tpu_custom_call" | custom-call | flops 4000000000 | bytes 4000000 | tf_op jit(solution)/shard_map/pallas_call | solution.py:390
  51.5 0.0 copy-start
  51.5 0.0 copy-start.2
  51.5 5.4 %all-to-all-done.1.got_ref = f32[32,3,4,128]{3,2,1,0:T(4,128)S(1)} async-done(((f32[32,3,4,128]{3,2,1,0:T(4,128)}), f32[32,3,4,128]{3,2,1,0:T(4,128)S(1)}, u32[]{:S(2)}, u32[]{:S(2)}) %all-to-all-start.1) | async-done | bytes 196640 | tf_op jit(solution)/shard_map/all_to_all | solution.py:370
  56.9 0.7 shard_map.96
  57.6 4.4 %all-to-all-start.2 = ((f32[32,8,128]{2,1,0:T(8,128)}), f32[32,8,128]{2,1,0:T(8,128)S(1)}, u32[]{:S(2)}, u32[]{:S(2)}) async-start(f32[32,8,128]{2,1,0:T(8,128)} %get-tuple-element.23), calls=%async_computation.2 | async-start | bytes 262144 | tf_op jit(solution)/shard_map/all_to_all | solution.py:370
  62.0 0.1 pad_add_fusion.index_ref
  62.1 0.0 copy-done
  62.1 0.0 copy-done.2
  62.1 2.0 %shard_map.97 = (f32[128,2048]{1,0:T(8,128)S(1)}, f32[64,128]{1,0:T(8,128)S(1)}, f32[128,128]{1,0:T(8,128)S(1)}, bf16[512,256]{1,0:T(8,128)(2,1)S(1)}, bf16[512,...) custom-call(s32[2]{0:T(128)S(1)} %pad_add_fusion.index_ref, ...), custom_call_target="tpu_custom_call" | custom-call | flops 1000000000 | bytes 8000000 | tf_op jit(solution)/shard_map/pallas_call | solution.py:403
  64.1 8.7 %all-to-all-done.2.got_ref = f32[32,8,128]{2,1,0:T(8,128)S(1)} async-done(((f32[32,8,128]{2,1,0:T(8,128)}), f32[32,8,128]{2,1,0:T(8,128)S(1)}, u32[]{:S(2)}, u32[]{:S(2)}) %all-to-all-start.2) | async-done | bytes 131104 | tf_op jit(solution)/shard_map/all_to_all | solution.py:370
  72.8 2.4 %shard_map.98 = bf16[16,144,128]{2,1,0:T(8,128)(2,1)S(1)} custom-call(s32[2]{0:T(128)S(1)} %pad_add_fusion.index_ref, f32[4]{0:T(128)S(1)} %copy-done.2, f32[32,8,128]{2,1,0:T(8,128)S(1)} %all-to-all-done.2.got_ref, f32[272,128]{1,0:T(8,128)S(1)} %get-tuple-element.24.middle_ref, s32[4,128]{1,0:T(4,128)S(1)} %bitcast.8, ...), custom_call_target="tpu_custom_call" | custom-call | tf_op jit(solution)/shard_map/pallas_call | solution.py:423
  75.2 22.5 %all_to_all.21.got_ref = bf16[16,144,128]{2,1,0:T(8,128)(2,1)S(1)} all-to-all(bf16[16,144,128]{2,1,0:T(8,128)(2,1)S(1)} %shard_map.98), channel_id=1, replica_groups=mesh['dp'=32,'clus'=16] {'clus'}, dimensions={0} | all-to-all | bytes 1179648 | tf_op jit(solution)/shard_map/all_to_all | solution.py:370
  97.6 1.1 %shard_map.99 = (bf16[256,1024]{1,0:T(8,128)(2,1)}, bf16[16,1024]{1,0:T(8,128)(2,1)}, bf16[1,1024]{1,0:T(2,128)(2,1)}, f32[2,128]{1,0:T(2,128)}) custom-call(bf16[16,144,128]{2,1,0:T(8,128)(2,1)S(1)} %all_to_all.21.got_ref, f32[8,128]{1,0:T(8,128)S(1)} %get-tuple-element.35.own_ref), custom_call_target="tpu_custom_call" | custom-call | tf_op jit(solution)/shard_map/pallas_call | solution.py:425
Async XLA Ops:
  0.6 28.6 %copy-start.1 = (s32[256]{0:T(256)S(1)}, s32[256]{0:T(256)}, u32[]{:S(2)}) copy-start(s32[256]{0:T(256)} %param.9) | copy-start | bytes 3076
  32.0 24.9 %all-to-all-start.1 = ((f32[32,3,4,128]{3,2,1,0:T(4,128)}), f32[32,3,4,128]{3,2,1,0:T(4,128)S(1)}, u32[]{:S(2)}, u32[]{:S(2)}) async-start(f32[32,3,4,128]{3,2,1,0:T(4,128)} %get-tuple-element.22), calls=%async_computation.1 | async-start | bytes 393216 | tf_op jit(solution)/shard_map/all_to_all | solution.py:370
  51.5 10.6 %copy-start = (s32[512]{0:T(512)S(1)}, s32[512]{0:T(512)}, u32[]{:S(2)}) copy-start(s32[512]{0:T(512)} %param.10) | copy-start | bytes 6148
  51.5 10.6 %copy-start.2 = (f32[4]{0:T(128)S(1)}, f32[4]{0:T(128)}, u32[]{:S(2)}) copy-start(f32[4]{0:T(128)} %shrink_ref.3) | copy-start | bytes 52
  57.6 15.2 %all-to-all-start.2 = ((f32[32,8,128]{2,1,0:T(8,128)}), f32[32,8,128]{2,1,0:T(8,128)S(1)}, u32[]{:S(2)}, u32[]{:S(2)}) async-start(f32[32,8,128]{2,1,0:T(8,128)} %get-tuple-element.23), calls=%async_computation.2 | async-start | bytes 262144 | tf_op jit(solution)/shard_map/all_to_all | solution.py:370

commit v5 on v4

--- a/solution.py
+++ b/solution.py
@@ -124,15 +124,14 @@
     second = hot(third + 256 == line)
     parts = side(middle, 2)
     sums = jnp.where(left, two(dot(first, parts)), two(dot(second, parts))).reshape(DP, 8, 128)
-    third_ref[:, 0] = sums[:, 0:4]
-    third_ref[:, 1] = sums[:, 4:8]
     high, low = pieces(tally, 2)
-    for k, ones in enumerate((first, second)):
-        count = dot_last(high, ones) + dot_last(low, ones)
-        for i in range(2):
-            third_ref[:, 2, 2 * k + i, :] = jnp.broadcast_to(
-                count[0:1, 128 * i : 128 * (i + 1)], (DP, 128)
-            )
+    counts = [dot_last(high, ones) + dot_last(low, ones) for ones in (first, second)]
+    counts = jnp.concatenate(
+        [count[0:1, 128 * i : 128 * (i + 1)] for count in counts for i in range(2)], axis=0
+    )
+    tail = jnp.concatenate([part.astype(F32) for part in pieces(counts, 2)], axis=0)
+    tail = jnp.broadcast_to(tail[None], (DP, 8, 128))
+    third_ref[...] = jnp.concatenate([sums, tail], axis=1).astype(BF)
 
 
 def fine_kernel(rows_ref, out_ref, ids_ref, wide_ref, acc_ref):
@@ -179,12 +178,11 @@
 
 
 def share_kernel(got_ref, acc_hbm, out_ref, count_ref):
-    total = got_ref[0]
+    total = got_ref[0].astype(F32)
     for k in range(1, DP):
-        total = total + got_ref[k]
-    sums = jnp.concatenate([total[0], total[1]], axis=0)
-    out_ref[...] = jnp.broadcast_to(sums[None], (DP, 8, 128))
-    count_ref[...] = total[2]
+        total = total + got_ref[k].astype(F32)
+    out_ref[...] = jnp.broadcast_to(total[None, 0:8], (DP, 8, 128))
+    count_ref[...] = total[8:12] + total[12:16]
 
 
 def ready_kernel(
@@ -383,7 +381,7 @@
         middle_kernel,
         24,
         [VMEM, ANY],
-        [((DP, 3, 4, 128), F32), ((272, 128), F32)],
+        [((DP, 16, 128), BF), ((272, 128), F32)],
         [pltpu.VMEM((512, 2048), BF), pltpu.VMEM((2, 128), I32), DMA],
     )(group_rows, parent2)
     third = exchange(third, "dp")

time: 99.1 us -> 99.1 us (level)
  waiting for transfers between devices: 14.1 us -> 12.8 us
  starting transfers between devices: 17.3 us -> 18.5 us
    all_to_all x2, waiting for transfers between devices: 14.1 us -> 12.8 us  [exchange(): return lax.all_to_all(x, axis, split_axis=0, concat_axis=0, tiled=True)]
    all_to_all x2, starting transfers between devices: 17.3 us -> 18.5 us  [exchange(): return lax.all_to_all(x, axis, split_axis=0, concat_axis=0, tiled=True)]
where the time goes in v5:
time: 99.1 us; the launch traced here: 98.7 us
  blocking collectives  49 us (49%)
  starting transfers between devices  18.5 us (19%)
  Pallas kernels  17.5 us (18%)
  waiting for transfers between devices  12.8 us (13%)
    all_to_all x2, blocking collectives, exchange(): return lax.all_to_all(x, axis, split_axis=0, concat_axis=0, tiled=True)  49 us
    all_to_all x2, starting transfers between devices, exchange(): return lax.all_to_all(x, axis, split_axis=0, concat_axis=0, tiled=True)  18.5 us
    all_to_all x2, waiting for transfers between devices, exchange(): return lax.all_to_all(x, axis, split_axis=0, concat_axis=0, tiled=True)  12.8 us
    pallas_call x1, Pallas kernels, local(): call(fine_kernel, 24, [VMEM], [((128, 2304), F32)], [pltpu.VMEM((128, 128...  6.59 us
    pallas_call x1, Pallas kernels, local(): call(middle_kernel, 24, [VMEM, ANY], [((DP, 16, 128), BF), ((272, 128), F...  2.7 us
    pallas_call x1, Pallas kernels, local(): call(down_kernel, 24, [SMEM, SMEM] + [VMEM] * 13, [block])  2.41 us
    pallas_call x1, Pallas kernels, local(): call(pack_kernel, 60, [VMEM] * 3, [block])  2.11 us
  transfers between devices with their start and end apart: 2, of which 2 were waited for; matrix products, arithmetic and copies ran while one was open for 0% of the time, Pallas kernels for 9%

profile of v5, /device:TPU:8, one launch (start us, length us, event | category | flops | bytes accessed | tf_op | source)
XLA Modules:
  0.0 98.7 jit_solution(4686002228054212676)
XLA Ops:
  0.6 0.0 copy-start.1
  0.6 2.1 %shard_map.93 = bf16[16,144,128]{2,1,0:T(8,128)(2,1)} custom-call(bf16[256,1024]{1,0:T(8,128)(2,1)} %rows_ref.1, s32[2,128]{1,0:T(2,128)} %bitcast.11, s32[2,128]{1,0:T(2,128)} %bitcast.12), custom_call_target="tpu_custom_call" | custom-call | tf_op jit(solution)/shard_map/pallas_call | solution.py:376
  2.8 26.5 %all_to_all.20.rows_ref = bf16[16,144,128]{2,1,0:T(8,128)(2,1)S(1)} all-to-all(bf16[16,144,128]{2,1,0:T(8,128)(2,1)} %shard_map.93), channel_id=1, replica_groups=mesh['dp'=32,'clus'=16] {'clus'}, dimensions={0} | all-to-all | bytes 1179648 | tf_op jit(solution)/shard_map/all_to_all | solution.py:368
  29.3 0.0 copy-done.1
  29.3 2.7 %shard_map.94 = (bf16[32,16,128]{2,1,0:T(8,128)(2,1)}, f32[272,128]{1,0:T(8,128)S(1)}) custom-call(bf16[16,144,128]{2,1,0:T(8,128)(2,1)S(1)} %all_to_all.20.rows_ref, s32[2,128]{1,0:T(2,128)S(1)} %bitcast.9), custom_call_target="tpu_custom_call" | custom-call | tf_op jit(solution)/shard_map/pallas_call | solution.py:380
  32.0 12.9 %all-to-all-start.1 = ((bf16[32,16,128]{2,1,0:T(8,128)(2,1)}), bf16[32,16,128]{2,1,0:T(8,128)(2,1)S(1)}, u32[]{:S(2)}, u32[]{:S(2)}) async-start(bf16[32,16,128]{2,1,0:T(8,128)(2,1)} %get-tuple-element.22), calls=%async_computation.1 | async-start | bytes 262144 | tf_op jit(solution)/shard_map/all_to_all | solution.py:368
  44.9 6.6 %shard_map.95.acc_hbm.acc_ref = f32[128,2304]{1,0:T(8,128)S(1)} custom-call(bf16[16,144,128]{2,1,0:T(8,128)(2,1)S(1)} %all_to_all.20.rows_ref), custom_call_target="tpu_custom_call" | custom-call | flops 4000000000 | bytes 4000000 | tf_op jit(solution)/shard_map/pallas_call | solution.py:388
  51.5 0.0 copy-start
  51.5 0.0 copy-start.2
  51.5 4.1 %all-to-all-done.1.got_ref = bf16[32,16,128]{2,1,0:T(8,128)(2,1)S(1)} async-done(((bf16[32,16,128]{2,1,0:T(8,128)(2,1)}), bf16[32,16,128]{2,1,0:T(8,128)(2,1)S(1)}, u32[]{:S(2)}, u32[]{:S(2)}) %all-to-all-start.1) | async-done | bytes 131104 | tf_op jit(solution)/shard_map/all_to_all | solution.py:368
  55.6 0.7 shard_map.96
  56.3 5.7 %all-to-all-start.2 = ((f32[32,8,128]{2,1,0:T(8,128)}), f32[32,8,128]{2,1,0:T(8,128)S(1)}, u32[]{:S(2)}, u32[]{:S(2)}) async-start(f32[32,8,128]{2,1,0:T(8,128)} %get-tuple-element.23), calls=%async_computation.2 | async-start | bytes 262144 | tf_op jit(solution)/shard_map/all_to_all | solution.py:368
  62.0 0.1 pad_add_fusion.index_ref
  62.1 0.0 copy-done
  62.1 0.0 copy-done.2
  62.1 2.0 %shard_map.97 = (f32[128,2048]{1,0:T(8,128)S(1)}, f32[64,128]{1,0:T(8,128)S(1)}, f32[128,128]{1,0:T(8,128)S(1)}, bf16[512,256]{1,0:T(8,128)(2,1)S(1)}, bf16[512,...) custom-call(s32[2]{0:T(128)S(1)} %pad_add_fusion.index_ref, ...), custom_call_target="tpu_custom_call" | custom-call | flops 1000000000 | bytes 8000000 | tf_op jit(solution)/shard_map/pallas_call | solution.py:401
  64.0 8.7 %all-to-all-done.2.got_ref = f32[32,8,128]{2,1,0:T(8,128)S(1)} async-done(((f32[32,8,128]{2,1,0:T(8,128)}), f32[32,8,128]{2,1,0:T(8,128)S(1)}, u32[]{:S(2)}, u32[]{:S(2)}) %all-to-all-start.2) | async-done | bytes 131104 | tf_op jit(solution)/shard_map/all_to_all | solution.py:368
  72.7 2.4 %shard_map.98 = bf16[16,144,128]{2,1,0:T(8,128)(2,1)S(1)} custom-call(s32[2]{0:T(128)S(1)} %pad_add_fusion.index_ref, f32[4]{0:T(128)S(1)} %copy-done.2, f32[32,8,128]{2,1,0:T(8,128)S(1)} %all-to-all-done.2.got_ref, f32[272,128]{1,0:T(8,128)S(1)} %get-tuple-element.24.middle_ref, s32[4,128]{1,0:T(4,128)S(1)} %bitcast.8, ...), custom_call_target="tpu_custom_call" | custom-call | tf_op jit(solution)/shard_map/pallas_call | solution.py:421
  75.2 22.5 %all_to_all.21.got_ref = bf16[16,144,128]{2,1,0:T(8,128)(2,1)S(1)} all-to-all(bf16[16,144,128]{2,1,0:T(8,128)(2,1)S(1)} %shard_map.98), channel_id=1, replica_groups=mesh['dp'=32,'clus'=16] {'clus'}, dimensions={0} | all-to-all | bytes 1179648 | tf_op jit(solution)/shard_map/all_to_all | solution.py:368
  97.6 1.1 %shard_map.99 = (bf16[256,1024]{1,0:T(8,128)(2,1)}, bf16[16,1024]{1,0:T(8,128)(2,1)}, bf16[1,1024]{1,0:T(2,128)(2,1)}, f32[2,128]{1,0:T(2,128)}) custom-call(bf16[16,144,128]{2,1,0:T(8,128)(2,1)S(1)} %all_to_all.21.got_ref, f32[8,128]{1,0:T(8,128)S(1)} %get-tuple-element.35.own_ref), custom_call_target="tpu_custom_call" | custom-call | tf_op jit(solution)/shard_map/pallas_call | solution.py:423
Async XLA Ops:
  0.6 28.6 %copy-start.1 = (s32[256]{0:T(256)S(1)}, s32[256]{0:T(256)}, u32[]{:S(2)}) copy-start(s32[256]{0:T(256)} %param.9) | copy-start | bytes 3076
  32.0 23.6 %all-to-all-start.1 = ((bf16[32,16,128]{2,1,0:T(8,128)(2,1)}), bf16[32,16,128]{2,1,0:T(8,128)(2,1)S(1)}, u32[]{:S(2)}, u32[]{:S(2)}) async-start(bf16[32,16,128]{2,1,0:T(8,128)(2,1)} %get-tuple-element.22), calls=%async_computation.1 | async-start | bytes 262144 | tf_op jit(solution)/shard_map/all_to_all | solution.py:368
  51.5 10.6 %copy-start = (s32[512]{0:T(512)S(1)}, s32[512]{0:T(512)}, u32[]{:S(2)}) copy-start(s32[512]{0:T(512)} %param.10) | copy-start | bytes 6148
  51.5 10.6 %copy-start.2 = (f32[4]{0:T(128)S(1)}, f32[4]{0:T(128)}, u32[]{:S(2)}) copy-start(f32[4]{0:T(128)} %shrink_ref.3) | copy-start | bytes 52
  56.3 16.4 %all-to-all-start.2 = ((f32[32,8,128]{2,1,0:T(8,128)}), f32[32,8,128]{2,1,0:T(8,128)S(1)}, u32[]{:S(2)}, u32[]{:S(2)}) async-start(f32[32,8,128]{2,1,0:T(8,128)} %get-tuple-element.23), calls=%async_computation.2 | async-start | bytes 262144 | tf_op jit(solution)/shard_map/all_to_all | solution.py:368

commit v6 on v5

--- a/solution.py
+++ b/solution.py
@@ -293,6 +293,7 @@
     lanes = (lane.astype(BF), (lane + 128.0).astype(BF))
     one, zero = jnp.array(1, BF), jnp.array(0, BF)
     halves = hot((iota((16, 256), 1) & 127) >> 6 == iota((16, 256), 0))
+    fourths = hot(iota((16, 256), 1) >> 6 == iota((16, 256), 0))
     for h in range(GROUPS):
         here = slice(128 * h, 128 * (h + 1))
         ones = []
@@ -307,12 +308,17 @@
         sums = acc_ref[:, here]
         fine = ((sums + weight_fine * prior) * inv_ref[:, here]).astype(BF)
         send_ref[h, 0:128, :] = fine
-        fine = fine.astype(F32)
-        spread = (
-            lines_ref[2 * h : 2 * h + 2]
-            + lines_ref[32 + 2 * h : 34 + 2 * h] * dot_last(halves, side(fine * fine, 2))[0:2]
-            - 2.0 * dot_last(halves, side(fine * sums, 2))[0:2]
-        )
+    for h in range(GROUPS):
+        here = slice(128 * h, 128 * (h + 1))
+        sums = acc_ref[:, here]
+        fine = send_ref[h, 0:128, :].astype(F32)
+        square = pieces(fine * fine, 3)
+        cross = pieces(fine * sums, 3)
+        last = dot_last(fourths, jnp.concatenate([square[2], cross[2]], axis=1))
+        square = dot_last(halves, jnp.concatenate(square[0:2], axis=1))[0:2] + last[0:2]
+        cross = dot_last(halves, jnp.concatenate(cross[0:2], axis=1))[0:2] + last[2:4]
+        counts = lines_ref[32 + 2 * h : 34 + 2 * h]
+        spread = lines_ref[2 * h : 2 * h + 2] + counts * square - 2.0 * cross
         send_ref[h, 128:144, :] = jnp.concatenate(
             [
                 jnp.where(

time: 99.1 us -> 99.2 us (level)
  no operation moved by 1% of the time
where the time goes in v6:
time: 99.2 us; the launch traced here: 98.8 us
  blocking collectives  49 us (49%)
  starting transfers between devices  18.5 us (19%)
  Pallas kernels  17.7 us (18%)
  waiting for transfers between devices  12.8 us (13%)
    all_to_all x2, blocking collectives, exchange(): return lax.all_to_all(x, axis, split_axis=0, concat_axis=0, tiled=True)  49 us
    all_to_all x2, starting transfers between devices, exchange(): return lax.all_to_all(x, axis, split_axis=0, concat_axis=0, tiled=True)  18.5 us
    all_to_all x2, waiting for transfers between devices, exchange(): return lax.all_to_all(x, axis, split_axis=0, concat_axis=0, tiled=True)  12.8 us
    pallas_call x1, Pallas kernels, local(): call(fine_kernel, 24, [VMEM], [((128, 2304), F32)], [pltpu.VMEM((128, 128...  6.59 us
    pallas_call x1, Pallas kernels, local(): call(middle_kernel, 24, [VMEM, ANY], [((DP, 16, 128), BF), ((272, 128), F...  2.7 us
    pallas_call x1, Pallas kernels, local(): call(down_kernel, 24, [SMEM, SMEM] + [VMEM] * 13, [block])  2.57 us
    pallas_call x1, Pallas kernels, local(): call(pack_kernel, 60, [VMEM] * 3, [block])  2.11 us
  transfers between devices with their start and end apart: 2, of which 2 were waited for; matrix products, arithmetic and copies ran while one was open for 0% of the time, Pallas kernels for 9%

profile of v6, /device:TPU:8, one launch (start us, length us, event | category | flops | bytes accessed | tf_op | source)
XLA Modules:
  0.0 98.8 jit_solution(5507323079416037340)
XLA Ops:
  0.6 0.0 copy-start.1
  0.6 2.1 %shard_map.93 = bf16[16,144,128]{2,1,0:T(8,128)(2,1)} custom-call(bf16[256,1024]{1,0:T(8,128)(2,1)} %rows_ref.1, s32[2,128]{1,0:T(2,128)} %bitcast.11, s32[2,128]{1,0:T(2,128)} %bitcast.12), custom_call_target="tpu_custom_call" | custom-call | tf_op jit(solution)/shard_map/pallas_call | solution.py:382
  2.8 26.5 %all_to_all.20.rows_ref = bf16[16,144,128]{2,1,0:T(8,128)(2,1)S(1)} all-to-all(bf16[16,144,128]{2,1,0:T(8,128)(2,1)} %shard_map.93), channel_id=1, replica_groups=mesh['dp'=32,'clus'=16] {'clus'}, dimensions={0} | all-to-all | bytes 1179648 | tf_op jit(solution)/shard_map/all_to_all | solution.py:374
  29.3 0.0 copy-done.1
  29.3 2.7 %shard_map.94 = (bf16[32,16,128]{2,1,0:T(8,128)(2,1)}, f32[272,128]{1,0:T(8,128)S(1)}) custom-call(bf16[16,144,128]{2,1,0:T(8,128)(2,1)S(1)} %all_to_all.20.rows_ref, s32[2,128]{1,0:T(2,128)S(1)} %bitcast.9), custom_call_target="tpu_custom_call" | custom-call | tf_op jit(solution)/shard_map/pallas_call | solution.py:386
  32.0 12.9 %all-to-all-start.1 = ((bf16[32,16,128]{2,1,0:T(8,128)(2,1)}), bf16[32,16,128]{2,1,0:T(8,128)(2,1)S(1)}, u32[]{:S(2)}, u32[]{:S(2)}) async-start(bf16[32,16,128]{2,1,0:T(8,128)(2,1)} %get-tuple-element.22), calls=%async_computation.1 | async-start | bytes 262144 | tf_op jit(solution)/shard_map/all_to_all | solution.py:374
  44.9 6.6 %shard_map.95.acc_hbm.acc_ref = f32[128,2304]{1,0:T(8,128)S(1)} custom-call(bf16[16,144,128]{2,1,0:T(8,128)(2,1)S(1)} %all_to_all.20.rows_ref), custom_call_target="tpu_custom_call" | custom-call | flops 4000000000 | bytes 4000000 | tf_op jit(solution)/shard_map/pallas_call | solution.py:394
  51.5 0.0 copy-start
  51.5 0.0 copy-start.2
  51.5 4.1 %all-to-all-done.1.got_ref = bf16[32,16,128]{2,1,0:T(8,128)(2,1)S(1)} async-done(((bf16[32,16,128]{2,1,0:T(8,128)(2,1)}), bf16[32,16,128]{2,1,0:T(8,128)(2,1)S(1)}, u32[]{:S(2)}, u32[]{:S(2)}) %all-to-all-start.1) | async-done | bytes 131104 | tf_op jit(solution)/shard_map/all_to_all | solution.py:374
  55.6 0.7 shard_map.96
  56.3 5.7 %all-to-all-start.2 = ((f32[32,8,128]{2,1,0:T(8,128)}), f32[32,8,128]{2,1,0:T(8,128)S(1)}, u32[]{:S(2)}, u32[]{:S(2)}) async-start(f32[32,8,128]{2,1,0:T(8,128)} %get-tuple-element.23), calls=%async_computation.2 | async-start | bytes 262144 | tf_op jit(solution)/shard_map/all_to_all | solution.py:374
  62.0 0.1 pad_add_fusion.index_ref
  62.1 0.0 copy-done
  62.1 0.0 copy-done.2
  62.1 2.0 %shard_map.97 = (f32[128,2048]{1,0:T(8,128)S(1)}, f32[64,128]{1,0:T(8,128)S(1)}, f32[128,128]{1,0:T(8,128)S(1)}, bf16[512,256]{1,0:T(8,128)(2,1)S(1)}, bf16[512,...) custom-call(s32[2]{0:T(128)S(1)} %pad_add_fusion.index_ref, ...), custom_call_target="tpu_custom_call" | custom-call | flops 1000000000 | bytes 8000000 | tf_op jit(solution)/shard_map/pallas_call | solution.py:407
  64.0 8.7 %all-to-all-done.2.got_ref = f32[32,8,128]{2,1,0:T(8,128)S(1)} async-done(((f32[32,8,128]{2,1,0:T(8,128)}), f32[32,8,128]{2,1,0:T(8,128)S(1)}, u32[]{:S(2)}, u32[]{:S(2)}) %all-to-all-start.2) | async-done | bytes 131104 | tf_op jit(solution)/shard_map/all_to_all | solution.py:374
  72.7 2.6 %shard_map.98 = bf16[16,144,128]{2,1,0:T(8,128)(2,1)S(1)} custom-call(s32[2]{0:T(128)S(1)} %pad_add_fusion.index_ref, f32[4]{0:T(128)S(1)} %copy-done.2, f32[32,8,128]{2,1,0:T(8,128)S(1)} %all-to-all-done.2.got_ref, f32[272,128]{1,0:T(8,128)S(1)} %get-tuple-element.24.middle_ref, s32[4,128]{1,0:T(4,128)S(1)} %bitcast.8, ...), custom_call_target="tpu_custom_call" | custom-call | tf_op jit(solution)/shard_map/pallas_call | solution.py:427
  75.3 22.5 %all_to_all.21.got_ref = bf16[16,144,128]{2,1,0:T(8,128)(2,1)S(1)} all-to-all(bf16[16,144,128]{2,1,0:T(8,128)(2,1)S(1)} %shard_map.98), channel_id=1, replica_groups=mesh['dp'=32,'clus'=16] {'clus'}, dimensions={0} | all-to-all | bytes 1179648 | tf_op jit(solution)/shard_map/all_to_all | solution.py:374
  97.8 1.1 %shard_map.99 = (bf16[256,1024]{1,0:T(8,128)(2,1)}, bf16[16,1024]{1,0:T(8,128)(2,1)}, bf16[1,1024]{1,0:T(2,128)(2,1)}, f32[2,128]{1,0:T(2,128)}) custom-call(bf16[16,144,128]{2,1,0:T(8,128)(2,1)S(1)} %all_to_all.21.got_ref, f32[8,128]{1,0:T(8,128)S(1)} %get-tuple-element.35.own_ref), custom_call_target="tpu_custom_call" | custom-call | tf_op jit(solution)/shard_map/pallas_call | solution.py:429
Async XLA Ops:
  0.6 28.6 %copy-start.1 = (s32[256]{0:T(256)S(1)}, s32[256]{0:T(256)}, u32[]{:S(2)}) copy-start(s32[256]{0:T(256)} %param.9) | copy-start | bytes 3076
  32.0 23.6 %all-to-all-start.1 = ((bf16[32,16,128]{2,1,0:T(8,128)(2,1)}), bf16[32,16,128]{2,1,0:T(8,128)(2,1)S(1)}, u32[]{:S(2)}, u32[]{:S(2)}) async-start(bf16[32,16,128]{2,1,0:T(8,128)(2,1)} %get-tuple-element.22), calls=%async_computation.1 | async-start | bytes 262144 | tf_op jit(solution)/shard_map/all_to_all | solution.py:374
  51.5 10.6 %copy-start = (s32[512]{0:T(512)S(1)}, s32[512]{0:T(512)}, u32[]{:S(2)}) copy-start(s32[512]{0:T(512)} %param.10) | copy-start | bytes 6148
  51.5 10.6 %copy-start.2 = (f32[4]{0:T(128)S(1)}, f32[4]{0:T(128)}, u32[]{:S(2)}) copy-start(f32[4]{0:T(128)} %shrink_ref.3) | copy-start | bytes 52
  56.3 16.4 %all-to-all-start.2 = ((f32[32,8,128]{2,1,0:T(8,128)}), f32[32,8,128]{2,1,0:T(8,128)S(1)}, u32[]{:S(2)}, u32[]{:S(2)}) async-start(f32[32,8,128]{2,1,0:T(8,128)} %get-tuple-element.23), calls=%async_computation.2 | async-start | bytes 262144 | tf_op jit(solution)/shard_map/all_to_all | solution.py:374

commit v7 on v4

--- a/solution.py
+++ b/solution.py
@@ -69,7 +69,7 @@
     return jnp.concatenate([ref[first + k : first + k + 1, :] for k in range(count)], axis=1)
 
 
-def pack_kernel(rows_ref, assign_ref, parent1_ref, send_ref):
+def pack_kernel(dp_ref, clus_ref, rows_ref, assign_ref, parent1_ref, send_ref):
     fine = assign_ref[...] & (GROUPS * FINE - 1)
     parent = parent1_ref[...] & (MIDDLE - 1)
     tile = jnp.concatenate(
@@ -135,7 +135,7 @@
             )
 
 
-def fine_kernel(rows_ref, out_ref, ids_ref, wide_ref, acc_ref):
+def fine_kernel(rows_ref, count_hbm, out_ref, ids_ref, wide_ref, acc_ref):
     lane = iota((128, 128), 1)
     left = lane < PART
     half = jnp.where(left, 0.0, 1.0)
@@ -178,7 +178,7 @@
             out_ref[:, 0:2176] = acc_ref[...] + part
 
 
-def share_kernel(got_ref, acc_hbm, out_ref, count_ref):
+def share_kernel(got_ref, out_ref, count_ref):
     total = got_ref[0]
     for k in range(1, DP):
         total = total + got_ref[k]
@@ -188,7 +188,7 @@
 
 
 def ready_kernel(
-    index_ref, shrink_ref, acc_ref, middle_ref, third_ref, parent2_ref, parent3_ref, inv_ref, lines_ref, cols_ref,
+    clus_ref, shrink_ref, acc_ref, middle_ref, third_ref, parent2_ref, parent3_ref, inv_ref, lines_ref, cols_ref,
     middle_turn_ref, top_turn_ref, third_inv_ref, top_inv_ref, down_ref, scale_ref, own_ref,
 ):
     weight_third = shrink_ref[1] * (TOTAL / THIRD)
@@ -201,7 +201,7 @@
     lines_ref[...] = lines[0:64]
     row = iota((32, 128), 0)
     own = [
-        jnp.sum(jnp.where(row == 2 * index_ref[1] + b, lines[32:64], 0.0), axis=0, keepdims=True)
+        jnp.sum(jnp.where(row == 2 * clus_ref[0] + b, lines[32:64], 0.0), axis=0, keepdims=True)
         for b in range(2)
     ]
     own_ref[...] = jnp.concatenate(own + [jnp.zeros((6, 128), F32)], axis=0)
@@ -259,7 +259,7 @@
 
 
 def down_kernel(
-    index_ref, shrink_ref, got_ref, middle_ref, parent3_ref, acc_ref, inv_ref, lines_ref, cols_ref, middle_turn_ref,
+    dp_ref, shrink_ref, got_ref, middle_ref, parent3_ref, acc_ref, inv_ref, lines_ref, cols_ref, middle_turn_ref,
     top_turn_ref, third_inv_ref, top_inv_ref, down_ref, scale_ref, send_ref,
 ):
     left = iota((256, 128), 1) < PART
@@ -282,7 +282,7 @@
     term = jnp.where(left, term[0:256], term[256:512])
     parts = side(top_means, 2)
     prior = term + turned(term) + scale_ref[...] * two(dot(down_ref[:, 0:TOP], parts))
-    index = index_ref[0]
+    index = dp_ref[0]
     rows = pl.ds(pl.multiple_of((index % 16) * 16, 16), 16)
     own = two(dot(top_turn_ref[pl.ds(pl.multiple_of(index * 16, 16), 16), 0:TOP], parts))
     own = (got_ref[pl.ds((index % 16) * 2, 2)].reshape(16, 128) + weight_third * own) * third_inv_ref[rows, :]
@@ -295,6 +295,7 @@
     lanes = (lane.astype(BF), (lane + 128.0).astype(BF))
     one, zero = jnp.array(1, BF), jnp.array(0, BF)
     halves = hot((iota((16, 256), 1) & 127) >> 6 == iota((16, 256), 0))
+    fourths = hot(iota((16, 256), 1) >> 6 == iota((16, 256), 0))
     for h in range(GROUPS):
         here = slice(128 * h, 128 * (h + 1))
         ones = []
@@ -309,12 +310,17 @@
         sums = acc_ref[:, here]
         fine = ((sums + weight_fine * prior) * inv_ref[:, here]).astype(BF)
         send_ref[h, 0:128, :] = fine
-        fine = fine.astype(F32)
-        spread = (
-            lines_ref[2 * h : 2 * h + 2]
-            + lines_ref[32 + 2 * h : 34 + 2 * h] * dot_last(halves, side(fine * fine, 2))[0:2]
-            - 2.0 * dot_last(halves, side(fine * sums, 2))[0:2]
-        )
+    for h in range(GROUPS):
+        here = slice(128 * h, 128 * (h + 1))
+        sums = acc_ref[:, here]
+        fine = send_ref[h, 0:128, :].astype(F32)
+        square = pieces(fine * fine, 3)
+        cross = pieces(fine * sums, 3)
+        last = dot_last(fourths, jnp.concatenate([square[2], cross[2]], axis=1))
+        square = dot_last(halves, jnp.concatenate(square[0:2], axis=1))[0:2] + last[0:2]
+        cross = dot_last(halves, jnp.concatenate(cross[0:2], axis=1))[0:2] + last[2:4]
+        counts = lines_ref[32 + 2 * h : 34 + 2 * h]
+        spread = lines_ref[2 * h : 2 * h + 2] + counts * square - 2.0 * cross
         send_ref[h, 128:144, :] = jnp.concatenate(
             [
                 jnp.where(
@@ -371,12 +377,13 @@
 
 
 def local(rows, fine_assign, parent1, parent2, parent3, shrink):
-    index = jnp.stack([lax.axis_index("dp"), lax.axis_index("clus")]).astype(I32)
+    dp = lax.axis_index("dp").astype(I32).reshape(1)
+    clus = lax.axis_index("clus").astype(I32).reshape(1)
     parent2 = parent2.reshape(2, 128)
     parent3 = parent3.reshape(4, 128)
     block = ((GROUPS, ROWS, 128), BF)
-    (send,) = call(pack_kernel, 60, [VMEM] * 3, [block])(
-        rows, fine_assign.reshape(2, 128), parent1.reshape(2, 128)
+    (send,) = call(pack_kernel, 60, [SMEM] * 2 + [VMEM] * 3, [block])(
+        dp, clus, rows, fine_assign.reshape(2, 128), parent1.reshape(2, 128)
     )
     group_rows = exchange(send, "clus")
     third, middle = call(
@@ -387,19 +394,17 @@
         [pltpu.VMEM((512, 2048), BF), pltpu.VMEM((2, 128), I32), DMA],
     )(group_rows, parent2)
     third = exchange(third, "dp")
+    third, counts = call(share_kernel, 24, [VMEM], [((DP, 8, 128), F32), ((4, 128), F32)])(third)
+    third = exchange(third, "dp")
     (sums,) = call(
         fine_kernel,
         24,
-        [VMEM],
+        [VMEM, ANY],
         [((128, 2304), F32)],
         [pltpu.VMEM((128, 128), F32), pltpu.VMEM((256, 2176), BF), pltpu.VMEM((128, 2176), F32)],
         4_000_000_000,
         4_000_000,
-    )(group_rows)
-    third, counts = call(share_kernel, 24, [VMEM, ANY], [((DP, 8, 128), F32), ((4, 128), F32)])(
-        third, sums
-    )
-    third = exchange(third, "dp")
+    )(group_rows, counts)
     *ready, own = call(
         ready_kernel,
         24,
@@ -419,8 +424,8 @@
         (),
         1_000_000_000,
         8_000_000,
-    )(index, shrink, sums, middle, counts, parent2, parent3)
-    (send,) = call(down_kernel, 24, [SMEM, SMEM] + [VMEM] * 13, [block])(index, shrink, third, middle, parent3, sums, *ready)
+    )(clus, shrink, sums, middle, counts, parent2, parent3)
+    (send,) = call(down_kernel, 24, [SMEM, SMEM] + [VMEM] * 13, [block])(dp, shrink, third, middle, parent3, sums, *ready)
     got = exchange(send, "clus")
     fine, middle, third, spread = call(
         finish_kernel,

time: 99.1 us -> 97.9 us (0.988)
  blocking collectives: 49 us -> 73.8 us
  starting transfers between devices: 17.3 us -> 3.86 us
  waiting for transfers between devices: 14.1 us -> 2.04 us
    all_to_all x2 -> x3, blocking collectives: 49 us -> 73.8 us  [exchange(): return lax.all_to_all(x, axis, split_axis=0, concat_axis=0, tiled=True)]
    all_to_all x2 -> x1, starting transfers between devices: 17.3 us -> 3.86 us  [exchange(): return lax.all_to_all(x, axis, split_axis=0, concat_axis=0, tiled=True)]
    all_to_all x2 -> x1, waiting for transfers between devices: 14.1 us -> 2.04 us  [exchange(): return lax.all_to_all(x, axis, split_axis=0, concat_axis=0, tiled=True)]
  transfers between devices with their start and end apart: 2 -> 1, of which waited for: 2 -> 1; matrix products, arithmetic and copies ran while one was open for 0% -> 0% of each run, Pallas kernels for 9% -> 9%
where the time goes in v7:
time: 97.9 us; the launch traced here: 97.6 us
  blocking collectives  73.8 us (75%)
  Pallas kernels  17.1 us (17%)
  starting transfers between devices  3.86 us (4%)
  waiting for transfers between devices  2.04 us (2%)
    all_to_all x3, blocking collectives, exchange(): return lax.all_to_all(x, axis, split_axis=0, concat_axis=0, tiled=True)  73.8 us
    pallas_call x1, Pallas kernels, local(): call(fine_kernel, 24, [VMEM, ANY], [((128, 2304), F32)], [pltpu.VMEM((128...  6.62 us
    all_to_all x1, starting transfers between devices, exchange(): return lax.all_to_all(x, axis, split_axis=0, concat_axis=0, tiled=True)  3.86 us
    pallas_call x1, Pallas kernels, local(): call(down_kernel, 24, [SMEM, SMEM] + [VMEM] * 13, [block])  2.58 us
    pallas_call x1, Pallas kernels, local(): call(pack_kernel, 60, [SMEM] * 2 + [VMEM] * 3, [block])  2.11 us
    pallas_call x1, Pallas kernels, local(): call(middle_kernel, 24, [VMEM, ANY], [((DP, 3, 4, 128), F32), ((272, 128)...  2.05 us
    all_to_all x1, waiting for transfers between devices, exchange(): return lax.all_to_all(x, axis, split_axis=0, concat_axis=0, tiled=True)  2.04 us
    pallas_call x1, Pallas kernels, local(): call(ready_kernel, 24, [SMEM, SMEM] + [VMEM] * 5, [((128, 2048), F32), ((...  1.98 us
  transfers between devices with their start and end apart: 1, of which 1 were waited for; matrix products, arithmetic and copies ran while one was open for 0% of the time, Pallas kernels for 9%

profile of v7, /device:TPU:8, one launch (start us, length us, event | category | flops | bytes accessed | tf_op | source)
XLA Modules:
  0.0 97.6 jit_solution(4908038316030368756)
XLA Ops:
  0.6 0.0 copy-start.1
  0.6 2.1 %shard_map.93 = bf16[16,144,128]{2,1,0:T(8,128)(2,1)} custom-call(s32[1]{0:T(128)} %bitcast.dp_ref, s32[1]{0:T(128)} %bitcast.1.clus_ref, bf16[256,1024]{1,0:T(8,128)(2,1)} %rows_ref.1, s32[2,128]{1,0:T(2,128)} %bitcast.11, s32[2,128]{1,0:T(2,128)} %bitcast.12), custom_call_target="tpu_custom_call" | custom-call | tf_op jit(solution)/shard_map/pallas_call | solution.py:385
  2.8 26.5 %all_to_all.20.rows_ref = bf16[16,144,128]{2,1,0:T(8,128)(2,1)S(1)} all-to-all(bf16[16,144,128]{2,1,0:T(8,128)(2,1)} %shard_map.93), channel_id=1, replica_groups=mesh['dp'=32,'clus'=16] {'clus'}, dimensions={0} | all-to-all | bytes 1179648 | tf_op jit(solution)/shard_map/all_to_all | solution.py:376
  29.3 0.0 copy-done.1
  29.3 2.0 %shard_map.94 = (f32[32,3,4,128]{3,2,1,0:T(4,128)S(1)}, f32[272,128]{1,0:T(8,128)S(1)}) custom-call(bf16[16,144,128]{2,1,0:T(8,128)(2,1)S(1)} %all_to_all.20.rows_ref, s32[2,128]{1,0:T(2,128)S(1)} %bitcast.9), custom_call_target="tpu_custom_call" | custom-call | tf_op jit(solution)/shard_map/pallas_call | solution.py:389
  31.3 24.7 %all_to_all.21.got_ref = f32[32,3,4,128]{3,2,1,0:T(4,128)S(1)} all-to-all(f32[32,3,4,128]{3,2,1,0:T(4,128)S(1)} %get-tuple-element.22), channel_id=1, replica_groups=mesh['dp'=32,'clus'=16] {'dp'}, dimensions={0} | all-to-all | bytes 393216 | tf_op jit(solution)/shard_map/all_to_all | solution.py:376
  56.0 0.7 shard_map.95
  56.7 3.9 %all-to-all-start.2 = ((f32[32,8,128]{2,1,0:T(8,128)}), f32[32,8,128]{2,1,0:T(8,128)S(1)}, u32[]{:S(2)}, u32[]{:S(2)}) async-start(f32[32,8,128]{2,1,0:T(8,128)} %get-tuple-element.23), calls=%async_computation.2 | async-start | bytes 262144 | tf_op jit(solution)/shard_map/all_to_all | solution.py:376
  60.6 0.0 copy-start
  60.6 0.0 copy-start.2
  60.6 6.6 %shard_map.96.acc_ref = f32[128,2304]{1,0:T(8,128)S(1)} custom-call(bf16[16,144,128]{2,1,0:T(8,128)(2,1)S(1)} %all_to_all.20.rows_ref, f32[4,128]{1,0:T(4,128)S(1)} %get-tuple-element.25.count_hbm.third_ref), custom_call_target="tpu_custom_call" | custom-call | flops 4000000000 | bytes 4000000 | tf_op jit(solution)/shard_map/pallas_call | solution.py:399
  67.2 0.0 copy-done
  67.2 0.0 copy-done.2
  67.3 2.0 %shard_map.97 = (f32[128,2048]{1,0:T(8,128)S(1)}, f32[64,128]{1,0:T(8,128)S(1)}, f32[128,128]{1,0:T(8,128)S(1)}, bf16[512,256]{1,0:T(8,128)(2,1)S(1)}, bf16[512,...) custom-call(s32[1]{0:T(128)} %bitcast.1.clus_ref, ...), custom_call_target="tpu_custom_call" | custom-call | flops 1000000000 | bytes 8000000 | tf_op jit(solution)/shard_map/pallas_call | solution.py:408
  69.2 2.0 %all-to-all-done.2.got_ref = f32[32,8,128]{2,1,0:T(8,128)S(1)} async-done(((f32[32,8,128]{2,1,0:T(8,128)}), f32[32,8,128]{2,1,0:T(8,128)S(1)}, u32[]{:S(2)}, u32[]{:S(2)}) %all-to-all-start.2) | async-done | bytes 131104 | tf_op jit(solution)/shard_map/all_to_all | solution.py:376
  71.3 2.6 %shard_map.98 = bf16[16,144,128]{2,1,0:T(8,128)(2,1)S(1)} custom-call(s32[1]{0:T(128)} %bitcast.dp_ref, f32[4]{0:T(128)S(1)} %copy-done.2, f32[32,8,128]{2,1,0:T(8,128)S(1)} %all-to-all-done.2.got_ref, f32[272,128]{1,0:T(8,128)S(1)} %get-tuple-element.24.middle_ref, s32[4,128]{1,0:T(4,128)S(1)} %bitcast.8, f32[128,2304]{1,0:T(8,128)S(1)} %shard_map.96.acc_ref, ...), custom_call_target="tpu_custom_call" | custom-call | tf_op jit(solution)/shard_map/pallas_call | solution.py:428
  73.9 22.6 %all_to_all.22.got_ref = bf16[16,144,128]{2,1,0:T(8,128)(2,1)S(1)} all-to-all(bf16[16,144,128]{2,1,0:T(8,128)(2,1)S(1)} %shard_map.98), channel_id=1, replica_groups=mesh['dp'=32,'clus'=16] {'clus'}, dimensions={0} | all-to-all | bytes 1179648 | tf_op jit(solution)/shard_map/all_to_all | solution.py:376
  96.5 1.1 %shard_map.99 = (bf16[256,1024]{1,0:T(8,128)(2,1)}, bf16[16,1024]{1,0:T(8,128)(2,1)}, bf16[1,1024]{1,0:T(2,128)(2,1)}, f32[2,128]{1,0:T(2,128)}) custom-call(bf16[16,144,128]{2,1,0:T(8,128)(2,1)S(1)} %all_to_all.22.got_ref, f32[8,128]{1,0:T(8,128)S(1)} %get-tuple-element.35.own_ref), custom_call_target="tpu_custom_call" | custom-call | tf_op jit(solution)/shard_map/pallas_call | solution.py:430
Async XLA Ops:
  0.6 28.7 %copy-start.1 = (s32[256]{0:T(256)S(1)}, s32[256]{0:T(256)}, u32[]{:S(2)}) copy-start(s32[256]{0:T(256)} %param.9) | copy-start | bytes 3076
  56.7 14.6 %all-to-all-start.2 = ((f32[32,8,128]{2,1,0:T(8,128)}), f32[32,8,128]{2,1,0:T(8,128)S(1)}, u32[]{:S(2)}, u32[]{:S(2)}) async-start(f32[32,8,128]{2,1,0:T(8,128)} %get-tuple-element.23), calls=%async_computation.2 | async-start | bytes 262144 | tf_op jit(solution)/shard_map/all_to_all | solution.py:376
  60.6 6.7 %copy-start = (s32[512]{0:T(512)S(1)}, s32[512]{0:T(512)}, u32[]{:S(2)}) copy-start(s32[512]{0:T(512)} %param.10) | copy-start | bytes 6148
  60.6 6.7 %copy-start.2 = (f32[4]{0:T(128)S(1)}, f32[4]{0:T(128)}, u32[]{:S(2)}) copy-start(f32[4]{0:T(128)} %shrink_ref.3) | copy-start | bytes 52

commit v8 on v7

--- a/solution.py
+++ b/solution.py
@@ -91,7 +91,7 @@
         send_ref[2 * g + 1, 128:144, :] = tile
 
 
-def middle_kernel(rows_ref, parent2_hbm, third_ref, middle_ref, hot_ref, parent2_ref, sem):
+def middle_kernel(rows_ref, parent2_hbm, down_hbm, third_ref, middle_ref, hot_ref, parent2_ref, sem):
     copy = pltpu.make_async_copy(parent2_hbm, parent2_ref, sem)
     copy.start()
     left = iota((256, 128), 1) < PART
@@ -135,7 +135,7 @@
             )
 
 
-def fine_kernel(rows_ref, count_hbm, out_ref, ids_ref, wide_ref, acc_ref):
+def fine_kernel(rows_ref, count_ref, out_ref, same_ref, ids_ref, wide_ref, acc_ref):
     lane = iota((128, 128), 1)
     left = lane < PART
     half = jnp.where(left, 0.0, 1.0)
@@ -143,6 +143,7 @@
     down = iota((128, 128), 0)
     for s in range(GROUPS):
         ids_ref[8 * s : 8 * s + 8, :] = rows_ref[s, 128:144, :].astype(F32)[0:8]
+    same_ref[...] = count_ref[...]
     columns = jnp.transpose(ids_ref[...])
     out_ref[:, 2176:2304] = columns
     for s in range(GROUPS):
@@ -187,9 +188,39 @@
     count_ref[...] = total[2]
 
 
+def parents_kernel(parent2_ref, parent3_ref, middle_turn_ref, top_turn_ref, down_ref):
+    cols = jnp.transpose(
+        jnp.concatenate(
+            [
+                jnp.zeros((2, 128), F32),
+                parent3_ref[...].astype(F32),
+                parent2_ref[...].astype(F32),
+                jnp.zeros((120, 128), F32),
+            ],
+            axis=0,
+        )
+    )
+    across = iota((128, 256), 1)
+    for k in range(2):
+        parent = cols[:, 6 + k : 7 + k].astype(I32)
+        for b in range(2):
+            middle_turn_ref[256 * b + 128 * k : 256 * b + 128 * (k + 1), :] = hot(
+                across + 256 * b == parent
+            )
+    for k in range(4):
+        top_turn_ref[128 * k : 128 * (k + 1), :] = hot(
+            across[:, 0:128] == cols[:, 2 + k : 3 + k].astype(I32)
+        )
+    down = jnp.zeros((256, 128), F32)
+    for b in range(2):
+        half = slice(256 * b, 256 * (b + 1))
+        down = down + dot(middle_turn_ref[half, :], top_turn_ref[half, :])
+    down_ref[...] = down.astype(BF)
+
+
 def ready_kernel(
-    clus_ref, shrink_ref, acc_ref, middle_ref, third_ref, parent2_ref, parent3_ref, inv_ref, lines_ref, cols_ref,
-    middle_turn_ref, top_turn_ref, third_inv_ref, top_inv_ref, down_ref, scale_ref, own_ref,
+    clus_ref, shrink_ref, acc_ref, middle_ref, third_ref, parent3_ref, middle_turn_ref, inv_ref, lines_ref, cols_ref,
+    third_inv_ref, top_inv_ref, scale_ref, own_ref,
 ):
     weight_third = shrink_ref[1] * (TOTAL / THIRD)
     weight_middle = shrink_ref[2] * (TOTAL / 8192)
@@ -216,8 +247,7 @@
             [
                 1.0 / (middle_ref[256:257, :] + weight_middle),
                 1.0 / (middle_ref[264:265, :] + weight_middle),
-                parent3_ref[...].astype(F32),
-                parent2_ref[...].astype(F32),
+                jnp.zeros((6, 128), F32),
                 1.0 / (third + weight_third),
                 jnp.zeros((116, 128), F32),
             ],
@@ -227,26 +257,12 @@
     third_inv_ref[...] = jnp.concatenate(
         [jnp.where(left, cols[:, 8 + k : 9 + k], cols[:, 10 + k : 11 + k]) for k in range(2)], axis=0
     )
-    across = iota((128, 256), 1)
-    for k in range(2):
-        parent = cols[:, 6 + k : 7 + k].astype(I32)
-        for b in range(2):
-            middle_turn_ref[256 * b + 128 * k : 256 * b + 128 * (k + 1), :] = hot(
-                across + 256 * b == parent
-            )
-    for k in range(4):
-        top_turn_ref[128 * k : 128 * (k + 1), :] = hot(
-            across[:, 0:128] == cols[:, 2 + k : 3 + k].astype(I32)
-        )
-    down = jnp.zeros((256, 128), F32)
     scale = jnp.zeros((256, 128), F32)
     for b in range(2):
         turn = middle_turn_ref[256 * b : 256 * (b + 1), :]
-        down = down + dot(turn, top_turn_ref[256 * b : 256 * (b + 1), :])
         column = jnp.concatenate([cols[:, 8 + 2 * b + k : 9 + 2 * b + k] for k in range(2)], axis=0)
         for part in pieces(jnp.broadcast_to(weight_third * column, (256, 128)), 3):
             scale = scale + dot(turn, part)
-    down_ref[...] = down.astype(BF)
     scale_ref[...] = scale
     ones = hot(iota((TOP, 512), 0) == in_line(parent3_ref, 0, 4))
     line = jnp.concatenate([third[k : k + 1] for k in range(4)], axis=1)
@@ -385,27 +401,36 @@
     (send,) = call(pack_kernel, 60, [SMEM] * 2 + [VMEM] * 3, [block])(
         dp, clus, rows, fine_assign.reshape(2, 128), parent1.reshape(2, 128)
     )
+    middle_turn, top_turn, down = call(
+        parents_kernel,
+        24,
+        [VMEM, VMEM],
+        [((2 * MIDDLE, 256), BF), ((THIRD, 128), BF), ((256, 128), BF)],
+        (),
+        1_000_000_000,
+        4_000_000,
+    )(parent2, parent3)
     group_rows = exchange(send, "clus")
     third, middle = call(
         middle_kernel,
         24,
-        [VMEM, ANY],
+        [VMEM, ANY, ANY],
         [((DP, 3, 4, 128), F32), ((272, 128), F32)],
         [pltpu.VMEM((512, 2048), BF), pltpu.VMEM((2, 128), I32), DMA],
-    )(group_rows, parent2)
+    )(group_rows, parent2, down)
     third = exchange(third, "dp")
     third, counts = call(share_kernel, 24, [VMEM], [((DP, 8, 128), F32), ((4, 128), F32)])(third)
     third = exchange(third, "dp")
-    (sums,) = call(
+    sums, counts = call(
         fine_kernel,
         24,
-        [VMEM, ANY],
-        [((128, 2304), F32)],
+        [VMEM, VMEM],
+        [((128, 2304), F32), ((4, 128), F32)],
         [pltpu.VMEM((128, 128), F32), pltpu.VMEM((256, 2176), BF), pltpu.VMEM((128, 2176), F32)],
         4_000_000_000,
         4_000_000,
     )(group_rows, counts)
-    *ready, own = call(
+    inv, lines, cols, third_inv, top_inv, scale, own = call(
         ready_kernel,
         24,
         [SMEM, SMEM] + [VMEM] * 5,
@@ -413,19 +438,18 @@
             ((128, 2048), F32),
             ((64, 128), F32),
             ((128, 128), F32),
-            ((2 * MIDDLE, 256), BF),
-            ((THIRD, 128), BF),
             ((256, 128), F32),
             ((TOP, 128), F32),
-            ((256, 128), BF),
             ((256, 128), F32),
             ((8, 128), F32),
         ],
         (),
         1_000_000_000,
         8_000_000,
-    )(clus, shrink, sums, middle, counts, parent2, parent3)
-    (send,) = call(down_kernel, 24, [SMEM, SMEM] + [VMEM] * 13, [block])(dp, shrink, third, middle, parent3, sums, *ready)
+    )(clus, shrink, sums, middle, counts, parent3, middle_turn)
+    (send,) = call(down_kernel, 24, [SMEM, SMEM] + [VMEM] * 13, [block])(
+        dp, shrink, third, middle, parent3, sums, inv, lines, cols, middle_turn, top_turn, third_inv, top_inv, down, scale
+    )
     got = exchange(send, "clus")
     fine, middle, third, spread = call(
         finish_kernel,

time: 97.9 us -> 96.8 us (0.989)
  blocking collectives: 73.8 us -> 47.8 us
  waiting for transfers between devices: 2.04 us -> 17.5 us
  starting transfers between devices: 3.86 us -> 13.1 us
    all_to_all x3 -> x2, blocking collectives: 73.8 us -> 47.8 us  [exchange(): return lax.all_to_all(x, axis, split_axis=0, concat_axis=0, tiled=True)]
    all_to_all x1 -> x2, waiting for transfers between devices: 2.04 us -> 17.5 us  [exchange(): return lax.all_to_all(x, axis, split_axis=0, concat_axis=0, tiled=True)]
    all_to_all x1 -> x2, starting transfers between devices: 3.86 us -> 13.1 us  [exchange(): return lax.all_to_all(x, axis, split_axis=0, concat_axis=0, tiled=True)]
    pallas_call x2 -> x3, Pallas kernels: 8.67 us -> 9.15 us  [the longest x1 6.6 us: local(): call(fine_kernel, 24, [VMEM, VMEM], [((128, 2304), F32), ((4, 128), F32)]...]
  transfers between devices with their start and end apart: 1 -> 2, of which waited for: 1 -> 2; matrix products, arithmetic and copies ran while one was open for 0% -> 0% of each run, Pallas kernels for 9% -> 9%
where the time goes in v8:
time: 96.8 us; the launch traced here: 96.5 us
  blocking collectives  47.8 us (49%)
  waiting for transfers between devices  17.5 us (18%)
  Pallas kernels  17.4 us (18%)
  starting transfers between devices  13.1 us (14%)
    all_to_all x2, blocking collectives, exchange(): return lax.all_to_all(x, axis, split_axis=0, concat_axis=0, tiled=True)  47.8 us
    all_to_all x2, waiting for transfers between devices, exchange(): return lax.all_to_all(x, axis, split_axis=0, concat_axis=0, tiled=True)  17.5 us
    all_to_all x2, starting transfers between devices, exchange(): return lax.all_to_all(x, axis, split_axis=0, concat_axis=0, tiled=True)  13.1 us
    pallas_call x1, Pallas kernels, local(): call(fine_kernel, 24, [VMEM, VMEM], [((128, 2304), F32), ((4, 128), F32)]...  6.6 us
    pallas_call x1, Pallas kernels, local(): call(down_kernel, 24, [SMEM, SMEM] + [VMEM] * 13, [block])  2.57 us
    pallas_call x1, Pallas kernels, local(): call(pack_kernel, 60, [SMEM] * 2 + [VMEM] * 3, [block])  2.12 us
    pallas_call x1, Pallas kernels, local(): call(middle_kernel, 24, [VMEM, ANY, ANY], [((DP, 3, 4, 128), F32), ((272,...  2.04 us
  transfers between devices with their start and end apart: 2, of which 2 were waited for; matrix products, arithmetic and copies ran while one was open for 0% of the time, Pallas kernels for 9%

profile of v8, /device:TPU:8, one launch (start us, length us, event | category | flops | bytes accessed | tf_op | source)
XLA Modules:
  0.0 96.5 jit_solution(12038936742181310736)
XLA Ops:
  0.6 0.0 copy-start
  0.6 0.0 copy-start.1
  0.7 2.1 %shard_map.93 = bf16[16,144,128]{2,1,0:T(8,128)(2,1)} custom-call(s32[1]{0:T(128)} %bitcast.dp_ref, s32[1]{0:T(128)} %bitcast.1.clus_ref, bf16[256,1024]{1,0:T(8,128)(2,1)} %rows_ref.1, s32[2,128]{1,0:T(2,128)} %bitcast.12, s32[2,128]{1,0:T(2,128)} %bitcast.13), custom_call_target="tpu_custom_call" | custom-call | tf_op jit(solution)/shard_map/pallas_call | solution.py:401
  2.8 9.2 %all-to-all-start = ((bf16[16,144,128]{2,1,0:T(8,128)(2,1)}), bf16[16,144,128]{2,1,0:T(8,128)(2,1)S(1)}, u32[]{:S(2)}, u32[]{:S(2)}) async-start(bf16[16,144,128]{2,1,0:T(8,128)(2,1)} %shard_map.93), calls=%async_computation | async-start | bytes 1179648 | tf_op jit(solution)/shard_map/all_to_all | solution.py:392
  12.0 0.0 copy-done
  12.0 0.0 copy-done.1
  12.0 0.5 shard_map.94
  12.5 15.2 %all-to-all-done.rows_ref = bf16[16,144,128]{2,1,0:T(8,128)(2,1)S(1)} async-done(((bf16[16,144,128]{2,1,0:T(8,128)(2,1)}), bf16[16,144,128]{2,1,0:T(8,128)(2,1)S(1)}, u32[]{:S(2)}, u32[]{:S(2)}) %all-to-all-start) | async-done | bytes 589856 | tf_op jit(solution)/shard_map/all_to_all | solution.py:392
  27.7 2.0 %shard_map.95 = (f32[32,3,4,128]{3,2,1,0:T(4,128)S(1)}, f32[272,128]{1,0:T(8,128)S(1)}) custom-call(bf16[16,144,128]{2,1,0:T(8,128)(2,1)S(1)} %all-to-all-done.rows_ref, s32[2,128]{1,0:T(2,128)S(1)} %bitcast.11, bf16[256,128]{1,0:T(8,128)(2,1)S(1)} %get-tuple-element.24.down_hbm.down_ref), custom_call_target="tpu_custom_call" | custom-call | tf_op jit(solution)/shard_map/pallas_call | solution.py:414
  29.8 24.5 %all_to_all.20.got_ref = f32[32,3,4,128]{3,2,1,0:T(4,128)S(1)} all-to-all(f32[32,3,4,128]{3,2,1,0:T(4,128)S(1)} %get-tuple-element.25), channel_id=1, replica_groups=mesh['dp'=32,'clus'=16] {'dp'}, dimensions={0} | all-to-all | bytes 393216 | tf_op jit(solution)/shard_map/all_to_all | solution.py:392
  54.3 0.7 shard_map.96
  55.0 3.9 %all-to-all-start.2 = ((f32[32,8,128]{2,1,0:T(8,128)}), f32[32,8,128]{2,1,0:T(8,128)S(1)}, u32[]{:S(2)}, u32[]{:S(2)}) async-start(f32[32,8,128]{2,1,0:T(8,128)} %get-tuple-element.26), calls=%async_computation.2 | async-start | bytes 262144 | tf_op jit(solution)/shard_map/all_to_all | solution.py:392
  58.8 0.0 copy-start.2
  58.9 6.6 %shard_map.97 = (f32[128,2304]{1,0:T(8,128)S(1)}, f32[4,128]{1,0:T(4,128)S(1)}) custom-call(bf16[16,144,128]{2,1,0:T(8,128)(2,1)S(1)} %all-to-all-done.rows_ref, f32[4,128]{1,0:T(4,128)S(1)} %get-tuple-element.28.count_ref), custom_call_target="tpu_custom_call" | custom-call | flops 4000000000 | bytes 4000000 | tf_op jit(solution)/shard_map/pallas_call | solution.py:424
  65.5 0.0 copy-done.2
  65.5 1.8 %shard_map.98 = (f32[128,2048]{1,0:T(8,128)S(1)}, f32[64,128]{1,0:T(8,128)S(1)}, f32[128,128]{1,0:T(8,128)S(1)}, f32[256,128]{1,0:T(8,128)S(1)}, f32[64,128]{1,0...) custom-call(s32[1]{0:T(128)} %bitcast.1.clus_ref, f32[4]{0:T(128)S(1)} %copy-done.2, ...), custom_call_target="tpu_custom_call" | custom-call | flops 1000000000 | bytes 8000000 | tf_op jit(solution)/shard_map/pallas_call | solution.py:433
  67.3 2.3 %all-to-all-done.2.got_ref = f32[32,8,128]{2,1,0:T(8,128)S(1)} async-done(((f32[32,8,128]{2,1,0:T(8,128)}), f32[32,8,128]{2,1,0:T(8,128)S(1)}, u32[]{:S(2)}, u32[]{:S(2)}) %all-to-all-start.2) | async-done | bytes 131104 | tf_op jit(solution)/shard_map/all_to_all | solution.py:392
  69.5 2.6 %shard_map.99 = bf16[16,144,128]{2,1,0:T(8,128)(2,1)S(1)} custom-call(s32[1]{0:T(128)} %bitcast.dp_ref, f32[4]{0:T(128)S(1)} %copy-done.2, f32[32,8,128]{2,1,0:T(8,128)S(1)} %all-to-all-done.2.got_ref, f32[272,128]{1,0:T(8,128)S(1)} %get-tuple-element.27.middle_ref, s32[4,128]{1,0:T(4,128)S(1)} %bitcast.9, f32[128,2304]{1,0:T(8,128)S(1)} %get-tuple-element.29.acc_ref, ...), custom_call_target="tpu_custom_call" | custom-call | tf_op jit(solution)/shard_map/pallas_call | solution.py:450
  72.1 23.3 %all_to_all.21.got_ref = bf16[16,144,128]{2,1,0:T(8,128)(2,1)S(1)} all-to-all(bf16[16,144,128]{2,1,0:T(8,128)(2,1)S(1)} %shard_map.99), channel_id=1, replica_groups=mesh['dp'=32,'clus'=16] {'clus'}, dimensions={0} | all-to-all | bytes 1179648 | tf_op jit(solution)/shard_map/all_to_all | solution.py:392
  95.4 1.1 %shard_map.100 = (bf16[256,1024]{1,0:T(8,128)(2,1)}, bf16[16,1024]{1,0:T(8,128)(2,1)}, bf16[1,1024]{1,0:T(2,128)(2,1)}, f32[2,128]{1,0:T(2,128)}) custom-call(bf16[16,144,128]{2,1,0:T(8,128)(2,1)S(1)} %all_to_all.21.got_ref, f32[8,128]{1,0:T(8,128)S(1)} %get-tuple-element.39.own_ref), custom_call_target="tpu_custom_call" | custom-call | tf_op jit(solution)/shard_map/pallas_call | solution.py:454
Async XLA Ops:
  0.6 11.3 %copy-start = (s32[512]{0:T(512)S(1)}, s32[512]{0:T(512)}, u32[]{:S(2)}) copy-start(s32[512]{0:T(512)} %param.10) | copy-start | bytes 6148
  0.6 11.3 %copy-start.1 = (s32[256]{0:T(256)S(1)}, s32[256]{0:T(256)}, u32[]{:S(2)}) copy-start(s32[256]{0:T(256)} %param.9) | copy-start | bytes 3076
  2.8 24.9 %all-to-all-start = ((bf16[16,144,128]{2,1,0:T(8,128)(2,1)}), bf16[16,144,128]{2,1,0:T(8,128)(2,1)S(1)}, u32[]{:S(2)}, u32[]{:S(2)}) async-start(bf16[16,144,128]{2,1,0:T(8,128)(2,1)} %shard_map.93), calls=%async_computation | async-start | bytes 1179648 | tf_op jit(solution)/shard_map/all_to_all | solution.py:392
  55.0 14.6 %all-to-all-start.2 = ((f32[32,8,128]{2,1,0:T(8,128)}), f32[32,8,128]{2,1,0:T(8,128)S(1)}, u32[]{:S(2)}, u32[]{:S(2)}) async-start(f32[32,8,128]{2,1,0:T(8,128)} %get-tuple-element.26), calls=%async_computation.2 | async-start | bytes 262144 | tf_op jit(solution)/shard_map/all_to_all | solution.py:392
  58.8 6.6 %copy-start.2 = (f32[4]{0:T(128)S(1)}, f32[4]{0:T(128)}, u32[]{:S(2)}) copy-start(f32[4]{0:T(128)} %shrink_ref.3) | copy-start | bytes 52
